TPU v7x, 256 devices: a whole 4x4x8 slice. The times are simulated.
256 devices in a mesh: coord: 64 (over x, z, core), dp: 4 (over y).
Axes of the slice: x: 4, y: 4, z: 8, core: 2. Of those that a mesh axis runs over, the one named last changes fastest.
Arguments:
- h_train: bfloat16 [2, 512, 256, 128], P(None, 'dp'), may hold values from -6 to 6
- gout_train: bfloat16 [2, 512, 256, 5120], P(None, 'dp', None, 'coord'), may hold values from -96 to 96
- h_val: bfloat16 [2, 64, 256, 128], P(None, 'dp'), may hold values from -6 to 6
- gout_val: bfloat16 [2, 64, 256, 5120], P(None, 'dp', None, 'coord'), may hold values from -96 to 96
- proj: bfloat16 [2, 5120, 128, 128], P(None, 'coord'), may hold values from -0.0390625 to 0.0390625
- bins: int32 [2, 5120], P(None, 'coord'), may hold values from 0 to 63
- tasks: int32 [64, 1], replicated, may hold values from 0 to 2
Outputs:
- cosines: float32 [512, 64], P('dp')
- scores: float32 [512, 3], P('dp')
Inputs may be any that keep to these rules, and one draw needn't show every extreme that they name: `tasks`: every one of the 3 benchmarks has at least one validation example.
All inputs are finite; a program needn't handle non-finite values.
Results may differ from a plain program's by a relative error of at most 0.0003.
Values sent between devices are 32-bit elements; how exact they have to be, the bound alone decides.
No kernel may reach another device: no remote copies, remote signals or barrier semaphores. Data moves between devices by JAX's collectives and lax.ppermute only.
A program may use at most 128 MiB of HBM per device.

v0:
```python
import jax
import jax.numpy as jnp
from jax import lax
from jax.sharding import PartitionSpec as P

KPROJ = 8192
BW = 128
NTASK = 3


def local_features(h_all, g_all, proj, bins):
    block_count = KPROJ // BW
    total = jnp.zeros((h_all.shape[1], block_count, BW), jnp.float32)
    for layer in range(h_all.shape[0]):
        grads = jnp.einsum(
            "etr,etj->ejr", h_all[layer], g_all[layer], preferred_element_type=jnp.float32
        ).astype(jnp.bfloat16)
        placed = jnp.einsum("ejr,jrk->ejk", grads, proj[layer], preferred_element_type=jnp.float32)
        onehot = (bins[layer][:, None] == jnp.arange(block_count)[None, :]).astype(jnp.float32)
        total = total + jnp.einsum("ejk,jb->ebk", placed, onehot, precision=lax.Precision.HIGHEST)
    return total.reshape(h_all.shape[1], block_count * BW)


def task_means(cosines, tasks):
    members = (tasks[:, 0][:, None] == jnp.arange(NTASK)[None, :]).astype(jnp.float32)
    return (
        jnp.dot(cosines, members, precision=lax.Precision.HIGHEST)
        / jnp.sum(members, axis=0)[None, :]
    )


def per_device(h_train, gout_train, h_val, gout_val, proj, bins, tasks):
    train_terms = local_features(h_train, gout_train, proj, bins)
    val_terms = local_features(h_val, gout_val, proj, bins)
    train_feats, val_local = lax.psum((train_terms, val_terms), "coord")
    val_feats = lax.all_gather(val_local, "dp", axis=0, tiled=True)
    train_norm = jnp.sqrt(jnp.sum(train_feats * train_feats, axis=1) + 1e-06)
    val_norm = jnp.sqrt(jnp.sum(val_feats * val_feats, axis=1) + 1e-06)
    dots = jnp.dot(train_feats, val_feats.T, precision=lax.Precision.HIGHEST)
    cosines = dots / (train_norm[:, None] * val_norm[None, :])
    return (cosines, task_means(cosines, tasks))


def solution(mesh):
    in_specs = (
        P(None, "dp", None, None),
        P(None, "dp", None, "coord"),
        P(None, "dp", None, None),
        P(None, "dp", None, "coord"),
        P(None, "coord", None, None),
        P(None, "coord"),
        P(),
    )
    out_specs = (P("dp", None), P("dp", None))
    return jax.shard_map(
        per_device, mesh=mesh, in_specs=in_specs, out_specs=out_specs, check_vma=False
    )
```

profile of v0, /device:TPU:1, one launch (start us, length us, event | category | flops | bytes accessed | tf_op | source)
XLA Modules:
  0.0 296.0 jit_solution(10054327431985492392)
XLA Ops:
  7.2 0.0 all-reduce.3.cloned.1.call-start
  7.2 0.0 slice-start
  7.2 6.8 %fusion.38 = bf16[128,80,128]{2,1,0:T(8,128)(2,1)S(1)} fusion(bf16[2,128,256,128]{3,2,1,0:T(8,128)(2,1)} %param.7, bf16[2,128,256,80]{2,3,1,0:T(8,128)(2,1)} %param.8), kind=kOutput, calls=%fused_computation.35 | convolution fusion | flops 672399360 | bytes 16252928 | tf_op jit(solution)/shard_map/etr,etj->ejr/dot_general | solution.py:15
  14.1 0.0 copy-start.2
  14.1 0.0 copy-start.3
  14.1 0.0 slice-start.1
  14.1 6.8 %fusion.33 = bf16[128,80,128]{2,1,0:T(8,128)(2,1)S(1)} fusion(bf16[2,128,256,128]{3,2,1,0:T(8,128)(2,1)} %param.7, bf16[2,128,256,80]{2,3,1,0:T(8,128)(2,1)} %param.8), kind=kOutput, calls=%fused_computation.34 | convolution fusion | flops 672399360 | bytes 16252928 | tf_op jit(solution)/shard_map/etr,etj->ejr/dot_general | solution.py:15
  20.9 0.0 copy-done.2
  21.0 0.0 copy-done.3
  21.0 0.0 copy-start.1
  21.0 0.3 convolution_convert_fusion.1
  21.3 0.3 convolution_convert_fusion
  21.7 0.0 copy-done.1
  21.7 0.0 slice-done
  21.7 0.0 slice-done.1
  21.7 0.9 fusion.18
  22.6 0.9 fusion.22
  23.5 5.8 %fusion.6 = f32[64,128,128]{2,0,1:T(8,128)S(1)} fusion(f32[80,128,128]{2,1,0:T(8,128)S(1)} %fusion.18, s32[80]{0:T(128)S(1)} %get-tuple-element.5), kind=kOutput, calls=%fused_computation.6 | convolution fusion | flops 1006638080 | bytes 9437504 | tf_op jit(solution)/shard_map/ejk,jb->ebk/dot_general | solution.py:20
  29.3 6.3 %fusion.30 = f32[64,128,128]{2,0,1:T(8,128)S(1)} fusion(f32[64,128,128]{2,0,1:T(8,128)S(1)} %fusion.6, f32[80,128,128]{2,1,0:T(8,128)S(1)} %fusion.22, s32[80]{0:T(128)S(1)} %get-tuple-element.4), kind=kOutput, calls=%fused_computation.32 | convolution fusion | flops 1007686656 | bytes 13631808 | tf_op jit(solution)/shard_map/ejk,jb->ebk/dot_general | solution.py:20
  35.5 5.3 %copy.47 = f32[16,8,64,128]{3,1,2,0:T(8,128)} copy(f32[16,8,64,128]{3,2,1,0:T(8,128)S(1)} %bitcast.85) | data formatting | bytes 8388608
  40.8 0.8 fusion.20
  41.6 0.6 fusion.49
  42.2 0.8 fusion.16
  43.0 0.0 copy-start.4
  43.0 0.6 convolution_add_fusion
  43.6 1.1 copy.48
  44.8 0.0 all-reduce.3.cloned.1.call-update
  44.8 0.3 all-gather.2.cloned.1.call-start
  45.1 198.5 %all-reduce.3.cloned.1.call-done = (f32[128,8192]{1,0:T(8,128)}, f32[16,8192]{1,0:T(8,128)}) async-done(((f32[128,8192]{1,0:T(8,128)}, f32[16,8192]{1,0:T(8,128)}), (f32[128,8192]{1,0:T(8,128)}, f32[16,8192]{1,0:T(8,128)})) %all-reduce.3.cloned.1.call-update) | async-done | bytes 4718608 | tf_op jit(solution)/shard_map/psum | solution.py:35
  243.5 0.0 all-gather.2.cloned.1.call-update
  243.6 0.0 copy-done.4
  243.6 0.1 convert_reduce_fusion
  243.7 2.5 multiply_reduce_fusion
  246.2 33.0 %all-gather.2.cloned.1.call-done = f32[64,8192]{1,0:T(8,128)} async-done(((f32[16,8192]{1,0:T(8,128)}), f32[64,8192]{1,0:T(8,128)}) %all-gather.2.cloned.1.call-update) | async-done | bytes 2097168 | tf_op jit(solution)/shard_map/all_gather | solution.py:36
  279.3 1.8 multiply_reduce_fusion.1
  281.1 7.3 %convolution_divide_fusion = f32[128,64]{0,1:T(8,128)S(1)} fusion(f32[128,8192]{1,0:T(8,128)} %get-tuple-element.2, f32[64,8192]{1,0:T(8,128)} %all-gather.2.cloned.1.call-done, f32[64]{0:T(128)S(1)} %add_sqrt_fusion, f32[128]{0:T(128)S(1)} %add_sqrt_fusion.1), kind=kOutput, calls=%fused_computation.39 | convolution fusion | flops 805322752 | bytes 6324992 | tf_op jit(solution)/shard_map/dot_general | solution.py:39
  288.4 0.0 copy-start
  288.4 0.7 convolution_divide_fusion.1
  289.1 0.0 copy-done
  (4 shorter events, 0.0 us)
Async XLA Ops:
  7.2 236.4 %all-reduce.3.cloned.1.call-start = ((), (), s32[]{:S(2)}) async-start(), calls=%async_computation.1 | async-start | bytes 9437184 | tf_op jit(solution)/shard_map/psum | solution.py:35
  7.2 14.5 %slice-start = ((s8[5242880]{0:T(1024)(128)(4,1)}), s8[4194304]{0:T(1024)(128)(4,1)S(1)}, s32[]{:S(2)}) async-start(s8[5242880]{0:T(1024)(128)(4,1)} %bitcast.82), calls=%async_computation.2 | async-start | bytes 8388608
  14.1 6.9 %copy-start.2 = (bf16[2,16,256,128]{3,2,1,0:T(8,128)(2,1)S(1)}, bf16[2,16,256,128]{3,2,1,0:T(8,128)(2,1)}, u32[]{:S(2)}) copy-start(bf16[2,16,256,128]{3,2,1,0:T(8,128)(2,1)} %param.9) | copy-start | bytes 6291460
  14.1 6.9 %copy-start.3 = (bf16[2,16,256,80]{2,3,1,0:T(8,128)(2,1)S(1)}, bf16[2,16,256,80]{2,3,1,0:T(8,128)(2,1)}, u32[]{:S(2)}) copy-start(bf16[2,16,256,80]{2,3,1,0:T(8,128)(2,1)} %param.10) | copy-start | bytes 3932164
  14.1 7.6 %slice-start.1 = ((s8[5242880]{0:T(1024)(128)(4,1)}), s8[1048576]{0:T(1024)(128)(4,1)S(1)}, s32[]{:S(2)}) async-start(s8[5242880]{0:T(1024)(128)(4,1)} %bitcast.82), calls=%async_computation.3 | async-start | bytes 2097152
  21.0 0.7 copy-start.1
  43.0 200.6 %copy-start.4 = (s32[64,1]{0,1:T(1,128)S(1)}, s32[64,1]{0,1:T(1,128)}, u32[]{:S(2)}) copy-start(s32[64,1]{0,1:T(1,128)} %param.13) | copy-start | bytes 772
  44.8 234.5 %all-gather.2.cloned.1.call-start = ((), (), s32[]{:S(2)}) async-start(), calls=%async_computation | async-start | bytes 2621440 | tf_op jit(solution)/shard_map/all_gather | solution.py:36
  288.4 0.7 copy-start
Sparse Core Ops, SparseCore 0:
  44.9 198.5 all-reduce.2
  245.5 33.7 all-gather.1
where the time goes:
time: 296 us
  waiting for transfers between devices  232 us (78%)
  matrix products  39 us (13%)
  between operations  14.2 us (5%)
  local copies, waits for them, and re-layouts  6.44 us (2%)
  other arithmetic  4.5 us (2%)
    psum x1, waiting for transfers between devices, per_device(): train_feats, val_local = lax.psum((train_terms, val_terms), 'coord')  198 us
    all_gather x1, waiting for transfers between devices, per_device(): val_feats = lax.all_gather(val_local, 'dp', axis=0, tiled=True)  33 us
    dot_general x4, matrix products, local_features(): jnp.einsum('etr,etj->ejr', h_all[layer], g_all[layer], preferred_element_...  14.3 us
    dot_general x4, matrix products, local_features(): jnp.einsum('ejk,jb->ebk', placed, onehot, precision=lax.Precision.HIGHEST)  13.3 us
    dot_general x1, matrix products, per_device(): dots = jnp.dot(train_feats, val_feats.T, precision=lax.Precision.HIGHEST)  7.28 us
    unnamed x16, local copies, waits for them, and re-layouts  6.44 us
  transfers between devices with their start and end apart: 2, of which 2 were waited for; matrix products, arithmetic and copies ran while one was open for 1% of the time, Pallas kernels for 0%

commit v1 on v0

v1 whole, which is shorter than its diff:
```python
import functools

import jax
import jax.numpy as jnp
from jax import lax
from jax.experimental import pallas as pl
from jax.experimental.pallas import tpu as pltpu
from jax.sharding import PartitionSpec as P

BW = 128
NTASK = 3
NBIN = 64
NX, NZ, NC, NY = 4, 8, 2, 4
HALF = NBIN // NC


def coord_pairs(target):
    place = lambda x, z, c: (x * NZ + z) * NC + c
    return [
        (place(x, z, c), place(*target(x, z, c)))
        for x in range(NX)
        for z in range(NZ)
        for c in range(NC)
    ]


def to_core(a):
    return lax.ppermute(a, "coord", coord_pairs(lambda x, z, c: (x, z, 1 - c)))


def along_x(a, d):
    return lax.ppermute(a, "coord", coord_pairs(lambda x, z, c: ((x + d) % NX, z, c)))


def along_z(a, d):
    return lax.ppermute(a, "coord", coord_pairs(lambda x, z, c: (x, (z + d) % NZ, c)))


def z_partner(a):
    return lax.ppermute(a, "coord", coord_pairs(lambda x, z, c: (x, z ^ 1, c)))


def along_y(a, d):
    return lax.ppermute(a, "dp", [(y, (y + d) % NY) for y in range(NY)])


def place_of_device():
    i = lax.axis_index("coord")
    return i // (NZ * NC), (i // NC) % NZ, i % NC


def feature_kernel(cfg, bins, h_t, g_t, h_v, g_v, proj, out, hbuf, gbuf, pbuf, grads, sem_t, sem_v, sem_p):
    layers, n_t, n_v, cols, blk, unroll_a, unroll_b = cfg
    n = n_t + n_v
    nblk = n_t // blk

    def copies_t(l, b):
        s = pl.ds(b * blk, blk)
        return (
            pltpu.make_async_copy(h_t.at[l, s], hbuf.at[l, s], sem_t.at[0, l, b]),
            pltpu.make_async_copy(g_t.at[l, s], gbuf.at[l, s], sem_t.at[1, l, b]),
        )

    def copies_v(l):
        s = pl.ds(n_t, n_v)
        return (
            pltpu.make_async_copy(h_v.at[l], hbuf.at[l, s], sem_v.at[0, l]),
            pltpu.make_async_copy(g_v.at[l], gbuf.at[l, s], sem_v.at[1, l]),
        )

    def copy_p(l):
        return pltpu.make_async_copy(proj.at[l], pbuf.at[l], sem_p.at[l])

    for l in range(layers):
        for copy in copies_v(l):
            copy.start()
        for b in range(nblk):
            for copy in copies_t(l, b):
                copy.start()
        copy_p(l).start()

    @pl.loop(0, NBIN)
    def _(b):
        out[b] = jnp.zeros((n, BW), jnp.float32)

    my_x, my_z, my_c = place_of_device()

    def example(l, e):
        g = jnp.dot(gbuf[l, e], hbuf[l, e], preferred_element_type=jnp.float32)
        grads[pl.ds(e, cols, stride=n), :] = g

    for l in range(layers):
        for copy in copies_v(l):
            copy.wait()

        @pl.loop(n_t, n, unroll=unroll_a)
        def _(e):
            example(l, e)

        @pl.loop(0, nblk)
        def _(b):
            for copy in copies_t(l, b):
                copy.wait()

            @pl.loop(0, blk, unroll=unroll_a)
            def _(e):
                example(l, b * blk + e)

        copy_p(l).wait()

        @pl.loop(0, cols, unroll=unroll_b)
        def _(j):
            a = grads[pl.ds(j * n, n), :].astype(jnp.bfloat16)
            p = jnp.dot(a, pbuf[l, j], preferred_element_type=jnp.float32)
            b = bins[l, j]
            far_c = (b // HALF) ^ my_c
            far_x = ((b // NZ) - my_x) & (NX - 1)
            far_z = (b - my_z) & (NZ - 1)
            out[far_c * HALF + far_x * NZ + far_z] += p


def local_features(bins, h_t, g_t, h_v, g_v, proj):
    layers, n_t, tok, r = h_t.shape
    n_v, cols = h_v.shape[1], g_t.shape[2]
    n = n_t + n_v
    blk = 16
    any_space = pl.BlockSpec(memory_space=pl.ANY)
    return pl.pallas_call(
        functools.partial(feature_kernel, (layers, n_t, n_v, cols, blk, 16, 16)),
        out_shape=jax.ShapeDtypeStruct((NBIN, n, BW), jnp.float32),
        in_specs=[pl.BlockSpec(memory_space=pltpu.SMEM)] + [any_space] * 5,
        out_specs=pl.BlockSpec(memory_space=pltpu.VMEM),
        scratch_shapes=[
            pltpu.VMEM((layers, n, tok, r), jnp.bfloat16),
            pltpu.VMEM((layers, n, cols, tok), jnp.bfloat16),
            pltpu.VMEM((layers, cols, r, BW), jnp.bfloat16),
            pltpu.VMEM((cols * n, r), jnp.float32),
            pltpu.SemaphoreType.DMA((2, layers, n_t // blk)),
            pltpu.SemaphoreType.DMA((2, layers)),
            pltpu.SemaphoreType.DMA((layers,)),
        ],
        compiler_params=pltpu.CompilerParams(vmem_limit_bytes=56 * 1024 * 1024),
        name="features",
    )(bins, h_t, g_t, h_v, g_v, proj)


def reduce_to_owner(f):
    half = {}
    for d in (2, 1, 3, 0):
        far = to_core(f[HALF + d * NZ : HALF + (d + 1) * NZ])
        half[d] = f[d * NZ : (d + 1) * NZ] + far
    mid = NZ // 2
    right = along_x(half[2][:mid], 1)
    left = along_x(half[2][mid:], -1)
    right = along_x(jnp.concatenate([half[1][:mid] + right, half[1][mid:]]), 1)
    left = along_x(jnp.concatenate([half[3][:mid], half[3][mid:] + left]), -1)
    own = half[0] + right + left
    got = [along_z(own[d], d) for d in (4, 3, 5, 2, 6, 1, 7)]
    total = own[0]
    for part in got:
        total = total + part
    return total


def dots_kernel(n_t, n_v, total, v1, v2, v3, keep, send, val, dots, stats):
    y = lax.axis_index("dp")
    _, _, c = place_of_device()
    train = total[0:n_t, :]
    val[pl.ds(pl.multiple_of(y * n_v, n_v), n_v), :] = total[n_t : n_t + n_v, :]
    for d, part in ((1, v1), (2, v2), (3, v3)):
        val[pl.ds(pl.multiple_of(((y - d) & (NY - 1)) * n_v, n_v), n_v), :] = part[...]
    v = val[...]
    contract = lambda a, b: lax.dot_general(
        a, b, (((1,), (1,)), ((), ())), precision=lax.Precision.HIGHEST, preferred_element_type=jnp.float32
    )
    dots[...] = contract(v, train)
    ones = jnp.ones((8, BW), jnp.float32)
    stats[0] = contract(ones, train * train)
    stats[1] = jnp.zeros_like(stats[1])
    stats[1, :, 0 : NY * n_v] = contract(ones, v * v)
    rows = NY * n_v // NC
    for ref, h in ((keep, c), (send, 1 - c)):
        ref[0:rows, :] = dots[pl.ds(pl.multiple_of(h * rows, rows), rows), :]
        ref[rows : rows + 8, :] = stats[h]


def scores_kernel(mine, other, tasks, cos_out, score_out, dots, stats):
    _, _, c = place_of_device()
    n_v = tasks.shape[1]
    rows = n_v // NC
    for ref, h in ((mine, c), (other, 1 - c)):
        dots[pl.ds(pl.multiple_of(h * rows, rows), rows), :] = ref[0:rows, :]
        stats[h] = ref[rows : rows + 8, :]
    on_diagonal = lax.broadcasted_iota(jnp.int32, (n_v, n_v), 0) == lax.broadcasted_iota(jnp.int32, (n_v, n_v), 1)
    train_norm = jnp.sqrt(stats[0, 0:1, :] + 1e-06)
    val_norm_row = jnp.sqrt(stats[1, 0:1, 0:n_v] + 1e-06)
    val_norm = jnp.sum(jnp.where(on_diagonal, val_norm_row, 0.0), axis=1, keepdims=True)
    cos = dots[...] / (train_norm * val_norm)
    cos_out[...] = cos
    task_row = tasks[...].astype(jnp.float32)
    task = jnp.sum(jnp.where(on_diagonal, task_row, 0.0), axis=1, keepdims=True)
    for s in range(NTASK):
        member = (task == float(s)).astype(jnp.float32)
        count = jnp.sum(member, axis=0, keepdims=True)
        score_out[s : s + 1, :] = jnp.sum(cos * member, axis=0, keepdims=True) / count


def per_device(h_train, gout_train, h_val, gout_val, proj, bins, tasks):
    n_t, n_v = h_train.shape[1], h_val.shape[1]
    all_v = n_v * NY
    f = local_features(
        bins, h_train, jnp.swapaxes(gout_train, 2, 3), h_val, jnp.swapaxes(gout_val, 2, 3), proj
    )
    total = reduce_to_owner(f)
    v = total[n_t:]
    others = [along_y(v, d) for d in (1, 2, 3)]
    part = jax.ShapeDtypeStruct((all_v // NC + 8, n_t), jnp.float32)
    keep, send = pl.pallas_call(
        functools.partial(dots_kernel, n_t, n_v),
        out_shape=(part, part),
        scratch_shapes=[
            pltpu.VMEM((all_v, BW), jnp.float32),
            pltpu.VMEM((all_v, n_t), jnp.float32),
            pltpu.VMEM((NC, 8, n_t), jnp.float32),
        ],
        name="dots",
    )(total, *others)
    a = keep + to_core(send)
    got = [along_x(a, d) for d in (2, 1, 3)]
    a = a + got[0] + got[1] + got[2]
    a = a + z_partner(a)
    got = [along_z(a, d) for d in (4, 2, 6)]
    a = a + got[0] + got[1] + got[2]
    cos_t, scores_t = pl.pallas_call(
        scores_kernel,
        out_shape=(
            jax.ShapeDtypeStruct((all_v, n_t), jnp.float32),
            jax.ShapeDtypeStruct((NTASK, n_t), jnp.float32),
        ),
        scratch_shapes=[
            pltpu.VMEM((all_v, n_t), jnp.float32),
            pltpu.VMEM((NC, 8, n_t), jnp.float32),
        ],
        name="scores",
    )(a, to_core(a), tasks.reshape(1, all_v))
    return cos_t.T, scores_t.T


def solution(mesh):
    in_specs = (
        P(None, "dp", None, None),
        P(None, "dp", None, "coord"),
        P(None, "dp", None, None),
        P(None, "dp", None, "coord"),
        P(None, "coord", None, None),
        P(None, "coord"),
        P(),
    )
    out_specs = (P("dp", None), P("dp", None))
    return jax.shard_map(
        per_device, mesh=mesh, in_specs=in_specs, out_specs=out_specs, check_vma=False
    )
```

time: 296 us -> 123 us (0.42)
  waiting for transfers between devices: 232 us -> 44.4 us
  starting transfers between devices: 0.3 us -> 47.3 us
  matrix products: 39 us -> 0 us
  Pallas kernels: 0 us -> 25.1 us
  between operations: 14.2 us -> 0.77 us
  other arithmetic: 4.5 us -> 1.36 us
    psum x1 -> x0, waiting for transfers between devices: 198 us -> none  [per_device(): train_feats, val_local = lax.psum((train_terms, val_terms), 'coord')]
    ppermute x0 -> x27, starting transfers between devices: none -> 47.3 us  [the longest x10 20.8 us: along_z(): lax.ppermute(a, 'coord', coord_pairs(lambda x, z, c: (x, (z + d) % NZ, c)))]
    ppermute x0 -> x27, waiting for transfers between devices: none -> 44.4 us  [the longest x7 25.6 us: along_x(): lax.ppermute(a, 'coord', coord_pairs(lambda x, z, c: ((x + d) % NX, z, c)))]
    dot_general x14 -> x0, matrix products: 39 us -> none  [the longest x4 14.3 us: local_features(): jnp.einsum('etr,etj->ejr', h_all[layer], g_all[layer], preferred_element_...]
    all_gather x1 -> x0, waiting for transfers between devices: 33 us -> none  [per_device(): val_feats = lax.all_gather(val_local, 'dp', axis=0, tiled=True)]
    pallas_call x0 -> x3, Pallas kernels: none -> 25.1 us  [the longest x1 21.7 us: local_features(): pl.pallas_call(functools.partial(feature_kernel, (layers, n_t, n_v, cols,...]
    unnamed x16 -> x14, local copies, waits for them, and re-layouts: 6.44 us -> 1.71 us
    reduce_sum x3 -> x0, other arithmetic: 4.48 us -> none  [the longest x1 2.54 us: per_device(): train_norm = jnp.sqrt(jnp.sum(train_feats * train_feats, axis=1) + 1e-06)]
  transfers between devices with their start and end apart: 2 -> 27, of which waited for: 2 -> 20; matrix products, arithmetic and copies ran while one was open for 1% -> 0% of each run, Pallas kernels for 0% -> 0%
where the time goes in v1:
time: 123 us
  starting transfers between devices  47.3 us (38%)
  waiting for transfers between devices  44.4 us (36%)
  Pallas kernels  25.1 us (20%)
  local copies, waits for them, and re-layouts  3.69 us (3%)
  other arithmetic  1.36 us (1%)
    ppermute x7, waiting for transfers between devices, along_x(): lax.ppermute(a, 'coord', coord_pairs(lambda x, z, c: ((x + d) % NX, z, c)))  25.6 us
    pallas_call x1, Pallas kernels, local_features(): pl.pallas_call(functools.partial(feature_kernel, (layers, n_t, n_v, cols,...  21.7 us
    ppermute x10, starting transfers between devices, along_z(): lax.ppermute(a, 'coord', coord_pairs(lambda x, z, c: (x, (z + d) % NZ, c)))  20.8 us
    ppermute x6, starting transfers between devices, to_core(): return lax.ppermute(a, 'coord', coord_pairs(lambda x, z, c: (x, z, 1 - c)))  14.8 us
    ppermute x10, waiting for transfers between devices, along_z(): lax.ppermute(a, 'coord', coord_pairs(lambda x, z, c: (x, (z + d) % NZ, c)))  9.92 us
    ppermute x7, starting transfers between devices, along_x(): lax.ppermute(a, 'coord', coord_pairs(lambda x, z, c: ((x + d) % NX, z, c)))  5.91 us
    ppermute x6, waiting for transfers between devices, to_core(): return lax.ppermute(a, 'coord', coord_pairs(lambda x, z, c: (x, z, 1 - c)))  4.71 us
    ppermute x3, starting transfers between devices, along_y(): return lax.ppermute(a, 'dp', [(y, (y + d) % NY) for y in range(NY)])  3.85 us
  transfers between devices with their start and end apart: 27, of which 20 were waited for; matrix products, arithmetic and copies ran while one was open for 0% of the time, Pallas kernels for 0%

profile of v1, /device:TPU:1, one launch (start us, length us, event | category | flops | bytes accessed | tf_op | source)
XLA Modules:
  0.0 122.6 jit_solution(10362025729252372363)
XLA Ops:
  0.6 21.7 %features.1 = f32[64,144,128]{2,1,0:T(8,128)} custom-call(s32[2,80]{1,0:T(2,128)} %bins.1, bf16[2,128,256,128]{3,2,1,0:T(8,128)(2,1)} %h_t.1, bf16[2,128,80,256]{3,2,1,0:T(8,128)(2,1)} %bitcast.35, bf16[2,16,256,128]{3,2,1,0:T(8,128)(2,1)} %h_v.1, bf16[2,16,80,256]{3,2,1,0:T(8,128)(2,1)} %bitcast.36, bf16[2,80,128,128]{3,2,1,0:T(8,128)(2,1)} %proj.1), custom_call_target="tpu_custom_call" | custom-call | tf_op jit(solution)/shard_map/features/pallas_call | solution.py:128
  22.3 1.9 %fusion.9 = (f32[8,144,128]{2,1,0:T(8,128)S(1)}, f32[8,144,128]{2,1,0:T(8,128)S(1)}, f32[8,144,128]{2,1,0:T(8,128)S(1)}, f32[8,144,128]{2,1,0:T(8,128)S(1)}) fusion(f32[64,144,128]{2,1,0:T(8,128)} %features.1), kind=kLoop, calls=%fused_computation.27 | loop fusion | bytes 4718592 | tf_op jit(solution)/shard_map/slice | solution.py:150
  24.3 3.3 %collective-permute-start.5 = (f32[8,144,128]{2,1,0:T(8,128)S(1)}, f32[8,144,128]{2,1,0:T(8,128)S(1)}, u32[]{:S(2)}, u32[]{:S(2)}) collective-permute-start(f32[8,144,128]{2,1,0:T(8,128)S(1)} %get-tuple-element.11), channel_id=1, source_target_pairs={{0,4},{4,0},{8,12},{12,8},{16,20},{20,16},{24,28},{28,24},{32,36},... | collective-permute-start | bytes 1769480 | tf_op jit(solution)/shard_map/ppermute | solution.py:28
  27.6 0.1 collective-permute-start.2
  27.7 0.4 collective-permute-start.1
  28.1 1.1 collective-permute-done.5
  29.2 0.8 collective-permute-done.2
  30.1 0.8 collective-permute-done.1
  30.9 0.2 slice_add_fusion.2
  31.1 0.8 collective-permute-start.6
  32.0 0.7 collective-permute-start
  32.6 0.7 collective-permute-start.3
  33.3 6.1 %collective-permute-done.6 = f32[4,144,128]{2,1,0:T(8,128)S(1)} collective-permute-done((f32[4,144,128]{2,1,0:T(8,128)S(1)}, f32[4,144,128]{2,1,0:T(8,128)S(1)}, u32[]{:S(2)}, u32[]{:S(2)}) %collective-permute-start.6) | collective-permute-done | bytes 294944 | tf_op jit(solution)/shard_map/ppermute | solution.py:32
  39.4 0.1 fusion.11
  39.6 2.0 %collective-permute-start.7 = (f32[8,144,128]{2,1,0:T(8,128)S(1)}, f32[8,144,128]{2,1,0:T(8,128)S(1)}, u32[]{:S(2)}, u32[]{:S(2)}) collective-permute-start(f32[8,144,128]{2,1,0:T(8,128)S(1)} %pad_maximum_fusion.1), channel_id=1, source_target_pairs={{0,192},{4,196},{8,200},{12,204},{16,208},{20,212},{24,216},{28,22... | collective-permute-start | bytes 1769480 | tf_op jit(solution)/shard_map/ppermute | solution.py:32
  41.6 0.9 collective-permute-done.3
  42.5 0.1 slice_add_fusion.5
  42.6 0.1 collective-permute-start.4
  42.7 0.0 collective-permute-done
  42.7 10.6 %collective-permute-done.7 = f32[8,144,128]{2,1,0:T(8,128)S(1)} collective-permute-done((f32[8,144,128]{2,1,0:T(8,128)S(1)}, f32[8,144,128]{2,1,0:T(8,128)S(1)}, u32[]{:S(2)}, u32[]{:S(2)}) %collective-permute-start.7) | collective-permute-done | bytes 589856 | tf_op jit(solution)/shard_map/ppermute | solution.py:32
  53.2 4.7 %collective-permute-done.4 = f32[8,144,128]{2,1,0:T(8,128)S(1)} collective-permute-done((f32[8,144,128]{2,1,0:T(8,128)S(1)}, f32[8,144,128]{2,1,0:T(8,128)S(1)}, u32[]{:S(2)}, u32[]{:S(2)}) %collective-permute-start.4) | collective-permute-done | bytes 589856 | tf_op jit(solution)/shard_map/ppermute | solution.py:32
  57.9 0.2 fusion.1
  58.2 7.0 %collective-permute-start.8 = (f32[144,128]{1,0:T(8,128)S(1)}, f32[144,128]{1,0:T(8,128)S(1)}, u32[]{:S(2)}, u32[]{:S(2)}) collective-permute-start(f32[144,128]{1,0:T(8,128)S(1)} %get-tuple-element.17), channel_id=1, source_target_pairs={{0,32},{4,36},{8,40},{12,44},{16,48},{20,52},{24,56},{28,60},{32,0... | collective-permute-start | bytes 221192 | tf_op jit(solution)/shard_map/ppermute | solution.py:36
  65.1 0.0 collective-permute-start.14
  65.2 1.5 %collective-permute-start.13 = (f32[144,128]{1,0:T(8,128)S(1)}, f32[144,128]{1,0:T(8,128)S(1)}, u32[]{:S(2)}, u32[]{:S(2)}) collective-permute-start(f32[144,128]{1,0:T(8,128)S(1)} %get-tuple-element.19), channel_id=1, source_target_pairs={{0,8},{4,12},{8,16},{12,20},{16,24},{20,28},{24,32},{28,36},{32,40... | collective-permute-start | bytes 221192 | tf_op jit(solution)/shard_map/ppermute | solution.py:36
  66.6 0.0 collective-permute-start.12
  66.6 2.4 %collective-permute-start.11 = (f32[144,128]{1,0:T(8,128)S(1)}, f32[144,128]{1,0:T(8,128)S(1)}, u32[]{:S(2)}, u32[]{:S(2)}) collective-permute-start(f32[144,128]{1,0:T(8,128)S(1)} %get-tuple-element.21), channel_id=1, source_target_pairs={{0,16},{4,20},{8,24},{12,28},{16,32},{20,36},{24,40},{28,44},{32,4... | collective-permute-start | bytes 221192 | tf_op jit(solution)/shard_map/ppermute | solution.py:36
  69.0 0.0 collective-permute-done.8
  69.0 3.0 %collective-permute-start.10 = (f32[144,128]{1,0:T(8,128)S(1)}, f32[144,128]{1,0:T(8,128)S(1)}, u32[]{:S(2)}, u32[]{:S(2)}) collective-permute-start(f32[144,128]{1,0:T(8,128)S(1)} %get-tuple-element.22), channel_id=1, source_target_pairs={{0,40},{4,44},{8,48},{12,52},{16,56},{20,60},{24,0},{28,4},{32,8},... | collective-permute-start | bytes 221192 | tf_op jit(solution)/shard_map/ppermute | solution.py:36
  72.0 0.0 collective-permute-done.14
  72.0 1.2 collective-permute-start.9
  73.1 0.0 collective-permute-done.13
  73.1 0.2 collective-permute-done.12
  73.4 0.0 collective-permute-done.11
  73.4 1.9 %collective-permute-done.10 = f32[144,128]{1,0:T(8,128)S(1)} collective-permute-done((f32[144,128]{1,0:T(8,128)S(1)}, f32[144,128]{1,0:T(8,128)S(1)}, u32[]{:S(2)}, u32[]{:S(2)}) %collective-permute-start.10) | collective-permute-done | bytes 73760 | tf_op jit(solution)/shard_map/ppermute | solution.py:36
  75.3 3.4 %collective-permute-done.9 = f32[144,128]{1,0:T(8,128)S(1)} collective-permute-done((f32[144,128]{1,0:T(8,128)S(1)}, f32[144,128]{1,0:T(8,128)S(1)}, u32[]{:S(2)}, u32[]{:S(2)}) %collective-permute-start.9) | collective-permute-done | bytes 73760 | tf_op jit(solution)/shard_map/ppermute | solution.py:36
  78.8 2.8 %collective-permute-start.17 = (f32[16,128]{1,0:T(8,128)S(1)}, f32[16,128]{1,0:T(8,128)S(1)}, u32[]{:S(2)}, u32[]{:S(2)}) collective-permute-start(f32[16,128]{1,0:T(8,128)S(1)} %slice.114), channel_id=1, source_target_pairs={{0,3},{1,0},{2,1},{3,2},{4,7},{5,4},{6,5},{7,6},{8,11},{9,8},{10,9... | collective-permute-start | bytes 24584 | tf_op jit(solution)/shard_map/ppermute | solution.py:44
  81.6 0.3 collective-permute-start.16
  82.0 0.7 collective-permute-start.15
  82.7 3.0 %collective-permute-done.16.v2 = f32[16,128]{1,0:T(8,128)S(1)} collective-permute-done((f32[16,128]{1,0:T(8,128)S(1)}, f32[16,128]{1,0:T(8,128)S(1)}, u32[]{:S(2)}, u32[]{:S(2)}) %collective-permute-start.16) | collective-permute-done | bytes 8224 | tf_op jit(solution)/shard_map/ppermute | solution.py:44
  85.6 0.1 collective-permute-done.15.v1
  85.7 0.5 copy-done.5
  86.2 0.6 copy-done.6
  86.8 1.9 %dots.1 = (f32[40,128]{1,0:T(8,128)}, f32[40,128]{1,0:T(8,128)}) custom-call(f32[144,128]{1,0:T(8,128)} %copy-done.1, f32[16,128]{1,0:T(8,128)} %copy-done.6, f32[16,128]{1,0:T(8,128)} %copy-done.5, f32[16,128]{1,0:T(8,128)} %copy-done.4), custom_call_target="tpu_custom_call" | custom-call | tf_op jit(solution)/shard_map/dots/pallas_call | solution.py:218
  88.7 5.5 %collective-permute-start.18 = (f32[40,128]{1,0:T(8,128)}, f32[40,128]{1,0:T(8,128)S(1)}, u32[]{:S(2)}, u32[]{:S(2)}) collective-permute-start(f32[40,128]{1,0:T(8,128)} %get-tuple-element.7), channel_id=1, source_target_pairs={{0,4},{4,0},{8,12},{12,8},{16,20},{20,16},{24,28},{28,24},{32,36},... | collective-permute-start | bytes 61448 | tf_op jit(solution)/shard_map/ppermute | solution.py:28
  94.3 1.1 collective-permute-done.18
  95.3 0.7 add.84
  96.0 0.0 collective-permute-start.21
  96.0 1.5 %collective-permute-start.20 = (f32[40,128]{1,0:T(8,128)S(1)}, f32[40,128]{1,0:T(8,128)S(1)}, u32[]{:S(2)}, u32[]{:S(2)}) collective-permute-start(f32[40,128]{1,0:T(8,128)S(1)} %add.84), channel_id=1, source_target_pairs={{0,64},{4,68},{8,72},{12,76},{16,80},{20,84},{24,88},{28,92},{32,9... | collective-permute-start | bytes 61448 | tf_op jit(solution)/shard_map/ppermute | solution.py:32
  97.5 0.8 collective-permute-start.19
  98.3 0.4 collective-permute-done.21
  98.7 1.2 collective-permute-done.20
  99.9 1.8 %collective-permute-done.19 = f32[40,128]{1,0:T(8,128)S(1)} collective-permute-done((f32[40,128]{1,0:T(8,128)S(1)}, f32[40,128]{1,0:T(8,128)S(1)}, u32[]{:S(2)}, u32[]{:S(2)}) %collective-permute-start.19) | collective-permute-done | bytes 20512 | tf_op jit(solution)/shard_map/ppermute | solution.py:32
  101.7 2.0 %collective-permute-start.22 = (f32[40,128]{1,0:T(8,128)S(1)}, f32[40,128]{1,0:T(8,128)S(1)}, u32[]{:S(2)}, u32[]{:S(2)}) collective-permute-start(f32[40,128]{1,0:T(8,128)S(1)} %add_add_fusion.1), channel_id=1, source_target_pairs={{0,8},{4,12},{8,0},{12,4},{16,24},{20,28},{24,16},{28,20},{32,40},... | collective-permute-start | bytes 61448 | tf_op jit(solution)/shard_map/ppermute | solution.py:40
  103.6 1.2 collective-permute-done.22
  104.8 3.6 %collective-permute-start.25 = (f32[40,128]{1,0:T(8,128)S(1)}, f32[40,128]{1,0:T(8,128)S(1)}, u32[]{:S(2)}, u32[]{:S(2)}) collective-permute-start(f32[40,128]{1,0:T(8,128)S(1)} %add.88), channel_id=1, source_target_pairs={{0,48},{4,52},{8,56},{12,60},{16,0},{20,4},{24,8},{28,12},{32,16},... | collective-permute-start | bytes 61448 | tf_op jit(solution)/shard_map/ppermute | solution.py:36
  108.4 0.0 collective-permute-start.24
  108.4 2.2 %collective-permute-start.23 = (f32[40,128]{1,0:T(8,128)S(1)}, f32[40,128]{1,0:T(8,128)S(1)}, u32[]{:S(2)}, u32[]{:S(2)}) collective-permute-start(f32[40,128]{1,0:T(8,128)S(1)} %add.88), channel_id=1, source_target_pairs={{0,32},{4,36},{8,40},{12,44},{16,48},{20,52},{24,56},{28,60},{32,0... | collective-permute-start | bytes 61448 | tf_op jit(solution)/shard_map/ppermute | solution.py:36
  110.6 2.5 %collective-permute-done.24 = f32[40,128]{1,0:T(8,128)S(1)} collective-permute-done((f32[40,128]{1,0:T(8,128)S(1)}, f32[40,128]{1,0:T(8,128)S(1)}, u32[]{:S(2)}, u32[]{:S(2)}) %collective-permute-start.24) | collective-permute-done | bytes 20512 | tf_op jit(solution)/shard_map/ppermute | solution.py:36
  113.1 1.8 %collective-permute-done.23 = f32[40,128]{1,0:T(8,128)S(1)} collective-permute-done((f32[40,128]{1,0:T(8,128)S(1)}, f32[40,128]{1,0:T(8,128)S(1)}, u32[]{:S(2)}, u32[]{:S(2)}) %collective-permute-start.23) | collective-permute-done | bytes 20512 | tf_op jit(solution)/shard_map/ppermute | solution.py:36
  114.9 4.7 %collective-permute-start.26 = (f32[40,128]{1,0:T(8,128)S(1)}, f32[40,128]{1,0:T(8,128)S(1)}, u32[]{:S(2)}, u32[]{:S(2)}) collective-permute-start(f32[40,128]{1,0:T(8,128)S(1)} %add_add_fusion.mine), channel_id=1, source_target_pairs={{0,4},{4,0},{8,12},{12,8},{16,20},{20,16},{24,28},{28,24},{32,36},... | collective-permute-start | bytes 61448 | tf_op jit(solution)/shard_map/ppermute | solution.py:28
  119.7 0.8 collective-permute-done.26.other
  120.5 0.6 copy-done.3
  121.1 1.5 %scores.1 = (f32[64,128]{1,0:T(8,128)}, f32[3,128]{1,0:T(4,128)}) custom-call(f32[40,128]{1,0:T(8,128)} %copy-done.2, f32[40,128]{1,0:T(8,128)} %copy-done.3, s32[1,64]{1,0:T(1,128)} %bitcast.37), custom_call_target="tpu_custom_call" | custom-call | tf_op jit(solution)/shard_map/scores/pallas_call | solution.py:234
  (22 shorter events, 0.2 us)
Async XLA Ops:
  22.3 8.6 %copy-start = (f32[64,144,128]{2,1,0:T(8,128)S(1)}, f32[64,144,128]{2,1,0:T(8,128)}, u32[]{:S(2)}) copy-start(f32[64,144,128]{2,1,0:T(8,128)} %features.1) | copy-start | bytes 14155780
  24.3 5.0 %collective-permute-start.5 = (f32[8,144,128]{2,1,0:T(8,128)S(1)}, f32[8,144,128]{2,1,0:T(8,128)S(1)}, u32[]{:S(2)}, u32[]{:S(2)}) collective-permute-start(f32[8,144,128]{2,1,0:T(8,128)S(1)} %get-tuple-element.11), channel_id=1, source_target_pairs={{0,4},{4,0},{8,12},{12,8},{16,20},{20,16},{24,28},{28,24},{32,36},... | collective-permute-start | bytes 1769480 | tf_op jit(solution)/shard_map/ppermute | solution.py:28
  27.6 2.5 %collective-permute-start.2 = (f32[8,144,128]{2,1,0:T(8,128)S(1)}, f32[8,144,128]{2,1,0:T(8,128)S(1)}, u32[]{:S(2)}, u32[]{:S(2)}) collective-permute-start(f32[8,144,128]{2,1,0:T(8,128)S(1)} %get-tuple-element.12), channel_id=1, source_target_pairs={{0,4},{4,0},{8,12},{12,8},{16,20},{20,16},{24,28},{28,24},{32,36},... | collective-permute-start | bytes 1769480 | tf_op jit(solution)/shard_map/ppermute | solution.py:28
  27.7 3.2 %collective-permute-start.1 = (f32[8,144,128]{2,1,0:T(8,128)S(1)}, f32[8,144,128]{2,1,0:T(8,128)S(1)}, u32[]{:S(2)}, u32[]{:S(2)}) collective-permute-start(f32[8,144,128]{2,1,0:T(8,128)S(1)} %get-tuple-element.13), channel_id=1, source_target_pairs={{0,4},{4,0},{8,12},{12,8},{16,20},{20,16},{24,28},{28,24},{32,36},... | collective-permute-start | bytes 1769480 | tf_op jit(solution)/shard_map/ppermute | solution.py:28
  31.1 8.3 %collective-permute-start.6 = (f32[4,144,128]{2,1,0:T(8,128)S(1)}, f32[4,144,128]{2,1,0:T(8,128)S(1)}, u32[]{:S(2)}, u32[]{:S(2)}) collective-permute-start(f32[4,144,128]{2,1,0:T(8,128)S(1)} %get-tuple-element.27), channel_id=1, source_target_pairs={{0,192},{4,196},{8,200},{12,204},{16,208},{20,212},{24,216},{28,22... | collective-permute-start | bytes 884744 | tf_op jit(solution)/shard_map/ppermute | solution.py:32
  32.0 10.7 %collective-permute-start = (f32[8,144,128]{2,1,0:T(8,128)S(1)}, f32[8,144,128]{2,1,0:T(8,128)S(1)}, u32[]{:S(2)}, u32[]{:S(2)}) collective-permute-start(f32[8,144,128]{2,1,0:T(8,128)S(1)} %get-tuple-element.10), channel_id=1, source_target_pairs={{0,4},{4,0},{8,12},{12,8},{16,20},{20,16},{24,28},{28,24},{32,36},... | collective-permute-start | bytes 1769480 | tf_op jit(solution)/shard_map/ppermute | solution.py:28
  32.6 9.8 %collective-permute-start.3 = (f32[4,144,128]{2,1,0:T(8,128)S(1)}, f32[4,144,128]{2,1,0:T(8,128)S(1)}, u32[]{:S(2)}, u32[]{:S(2)}) collective-permute-start(f32[4,144,128]{2,1,0:T(8,128)S(1)} %get-tuple-element.26), channel_id=1, source_target_pairs={{0,64},{4,68},{8,72},{12,76},{16,80},{20,84},{24,88},{28,92},{32,9... | collective-permute-start | bytes 884744 | tf_op jit(solution)/shard_map/ppermute | solution.py:32
  39.6 13.7 %collective-permute-start.7 = (f32[8,144,128]{2,1,0:T(8,128)S(1)}, f32[8,144,128]{2,1,0:T(8,128)S(1)}, u32[]{:S(2)}, u32[]{:S(2)}) collective-permute-start(f32[8,144,128]{2,1,0:T(8,128)S(1)} %pad_maximum_fusion.1), channel_id=1, source_target_pairs={{0,192},{4,196},{8,200},{12,204},{16,208},{20,212},{24,216},{28,22... | collective-permute-start | bytes 1769480 | tf_op jit(solution)/shard_map/ppermute | solution.py:32
  42.6 15.4 %collective-permute-start.4 = (f32[8,144,128]{2,1,0:T(8,128)S(1)}, f32[8,144,128]{2,1,0:T(8,128)S(1)}, u32[]{:S(2)}, u32[]{:S(2)}) collective-permute-start(f32[8,144,128]{2,1,0:T(8,128)S(1)} %pad_maximum_fusion), channel_id=1, source_target_pairs={{0,64},{4,68},{8,72},{12,76},{16,80},{20,84},{24,88},{28,92},{32,9... | collective-permute-start | bytes 1769480 | tf_op jit(solution)/shard_map/ppermute | solution.py:32
  58.2 10.8 %collective-permute-start.8 = (f32[144,128]{1,0:T(8,128)S(1)}, f32[144,128]{1,0:T(8,128)S(1)}, u32[]{:S(2)}, u32[]{:S(2)}) collective-permute-start(f32[144,128]{1,0:T(8,128)S(1)} %get-tuple-element.17), channel_id=1, source_target_pairs={{0,32},{4,36},{8,40},{12,44},{16,48},{20,52},{24,56},{28,60},{32,0... | collective-permute-start | bytes 221192 | tf_op jit(solution)/shard_map/ppermute | solution.py:36
  65.1 6.8 %collective-permute-start.14 = (f32[144,128]{1,0:T(8,128)S(1)}, f32[144,128]{1,0:T(8,128)S(1)}, u32[]{:S(2)}, u32[]{:S(2)}) collective-permute-start(f32[144,128]{1,0:T(8,128)S(1)} %get-tuple-element.18), channel_id=1, source_target_pairs={{0,56},{4,60},{8,0},{12,4},{16,8},{20,12},{24,16},{28,20},{32,24},... | collective-permute-start | bytes 221192 | tf_op jit(solution)/shard_map/ppermute | solution.py:36
  65.2 8.0 %collective-permute-start.13 = (f32[144,128]{1,0:T(8,128)S(1)}, f32[144,128]{1,0:T(8,128)S(1)}, u32[]{:S(2)}, u32[]{:S(2)}) collective-permute-start(f32[144,128]{1,0:T(8,128)S(1)} %get-tuple-element.19), channel_id=1, source_target_pairs={{0,8},{4,12},{8,16},{12,20},{16,24},{20,28},{24,32},{28,36},{32,40... | collective-permute-start | bytes 221192 | tf_op jit(solution)/shard_map/ppermute | solution.py:36
  66.6 6.8 %collective-permute-start.12 = (f32[144,128]{1,0:T(8,128)S(1)}, f32[144,128]{1,0:T(8,128)S(1)}, u32[]{:S(2)}, u32[]{:S(2)}) collective-permute-start(f32[144,128]{1,0:T(8,128)S(1)} %get-tuple-element.20), channel_id=1, source_target_pairs={{0,48},{4,52},{8,56},{12,60},{16,0},{20,4},{24,8},{28,12},{32,16},... | collective-permute-start | bytes 221192 | tf_op jit(solution)/shard_map/ppermute | solution.py:36
  66.6 6.8 %collective-permute-start.11 = (f32[144,128]{1,0:T(8,128)S(1)}, f32[144,128]{1,0:T(8,128)S(1)}, u32[]{:S(2)}, u32[]{:S(2)}) collective-permute-start(f32[144,128]{1,0:T(8,128)S(1)} %get-tuple-element.21), channel_id=1, source_target_pairs={{0,16},{4,20},{8,24},{12,28},{16,32},{20,36},{24,40},{28,44},{32,4... | collective-permute-start | bytes 221192 | tf_op jit(solution)/shard_map/ppermute | solution.py:36
  69.0 6.3 %collective-permute-start.10 = (f32[144,128]{1,0:T(8,128)S(1)}, f32[144,128]{1,0:T(8,128)S(1)}, u32[]{:S(2)}, u32[]{:S(2)}) collective-permute-start(f32[144,128]{1,0:T(8,128)S(1)} %get-tuple-element.22), channel_id=1, source_target_pairs={{0,40},{4,44},{8,48},{12,52},{16,56},{20,60},{24,0},{28,4},{32,8},... | collective-permute-start | bytes 221192 | tf_op jit(solution)/shard_map/ppermute | solution.py:36
  72.0 6.8 %collective-permute-start.9 = (f32[144,128]{1,0:T(8,128)S(1)}, f32[144,128]{1,0:T(8,128)S(1)}, u32[]{:S(2)}, u32[]{:S(2)}) collective-permute-start(f32[144,128]{1,0:T(8,128)S(1)} %get-tuple-element.23), channel_id=1, source_target_pairs={{0,24},{4,28},{8,32},{12,36},{16,40},{20,44},{24,48},{28,52},{32,5... | collective-permute-start | bytes 221192 | tf_op jit(solution)/shard_map/ppermute | solution.py:36
  78.8 6.9 %copy-start.1 = (f32[144,128]{1,0:T(8,128)}, f32[144,128]{1,0:T(8,128)S(1)}, u32[]{:S(2)}) copy-start(f32[144,128]{1,0:T(8,128)S(1)} %fusion.8.total) | copy-start | bytes 221188
  78.8 3.9 %collective-permute-start.17 = (f32[16,128]{1,0:T(8,128)S(1)}, f32[16,128]{1,0:T(8,128)S(1)}, u32[]{:S(2)}, u32[]{:S(2)}) collective-permute-start(f32[16,128]{1,0:T(8,128)S(1)} %slice.114), channel_id=1, source_target_pairs={{0,3},{1,0},{2,1},{3,2},{4,7},{5,4},{6,5},{7,6},{8,11},{9,8},{10,9... | collective-permute-start | bytes 24584 | tf_op jit(solution)/shard_map/ppermute | solution.py:44
  81.6 4.0 %collective-permute-start.16 = (f32[16,128]{1,0:T(8,128)S(1)}, f32[16,128]{1,0:T(8,128)S(1)}, u32[]{:S(2)}, u32[]{:S(2)}) collective-permute-start(f32[16,128]{1,0:T(8,128)S(1)} %slice.114), channel_id=1, source_target_pairs={{0,2},{1,3},{2,0},{3,1},{4,6},{5,7},{6,4},{7,5},{8,10},{9,11},{10,... | collective-permute-start | bytes 24584 | tf_op jit(solution)/shard_map/ppermute | solution.py:44
  82.0 3.7 %collective-permute-start.15 = (f32[16,128]{1,0:T(8,128)S(1)}, f32[16,128]{1,0:T(8,128)S(1)}, u32[]{:S(2)}, u32[]{:S(2)}) collective-permute-start(f32[16,128]{1,0:T(8,128)S(1)} %slice.114), channel_id=1, source_target_pairs={{0,1},{1,2},{2,3},{3,0},{4,5},{5,6},{6,7},{7,4},{8,9},{9,10},{10,1... | collective-permute-start | bytes 24584 | tf_op jit(solution)/shard_map/ppermute | solution.py:44
  82.7 3.1 %copy-start.4 = (f32[16,128]{1,0:T(8,128)}, f32[16,128]{1,0:T(8,128)S(1)}, u32[]{:S(2)}) copy-start(f32[16,128]{1,0:T(8,128)S(1)} %collective-permute-done.17.v3) | copy-start | bytes 24580
  85.6 0.6 copy-start.5
  86.2 0.6 copy-start.6
  88.7 6.6 %collective-permute-start.18 = (f32[40,128]{1,0:T(8,128)}, f32[40,128]{1,0:T(8,128)S(1)}, u32[]{:S(2)}, u32[]{:S(2)}) collective-permute-start(f32[40,128]{1,0:T(8,128)} %get-tuple-element.7), channel_id=1, source_target_pairs={{0,4},{4,0},{8,12},{12,8},{16,20},{20,16},{24,28},{28,24},{32,36},... | collective-permute-start | bytes 61448 | tf_op jit(solution)/shard_map/ppermute | solution.py:28
  96.0 2.6 %collective-permute-start.21 = (f32[40,128]{1,0:T(8,128)S(1)}, f32[40,128]{1,0:T(8,128)S(1)}, u32[]{:S(2)}, u32[]{:S(2)}) collective-permute-start(f32[40,128]{1,0:T(8,128)S(1)} %add.84), channel_id=1, source_target_pairs={{0,192},{4,196},{8,200},{12,204},{16,208},{20,212},{24,216},{28,22... | collective-permute-start | bytes 61448 | tf_op jit(solution)/shard_map/ppermute | solution.py:32
  96.0 3.8 %collective-permute-start.20 = (f32[40,128]{1,0:T(8,128)S(1)}, f32[40,128]{1,0:T(8,128)S(1)}, u32[]{:S(2)}, u32[]{:S(2)}) collective-permute-start(f32[40,128]{1,0:T(8,128)S(1)} %add.84), channel_id=1, source_target_pairs={{0,64},{4,68},{8,72},{12,76},{16,80},{20,84},{24,88},{28,92},{32,9... | collective-permute-start | bytes 61448 | tf_op jit(solution)/shard_map/ppermute | solution.py:32
  97.5 4.1 %collective-permute-start.19 = (f32[40,128]{1,0:T(8,128)S(1)}, f32[40,128]{1,0:T(8,128)S(1)}, u32[]{:S(2)}, u32[]{:S(2)}) collective-permute-start(f32[40,128]{1,0:T(8,128)S(1)} %add.84), channel_id=1, source_target_pairs={{0,128},{4,132},{8,136},{12,140},{16,144},{20,148},{24,152},{28,15... | collective-permute-start | bytes 61448 | tf_op jit(solution)/shard_map/ppermute | solution.py:32
  101.7 3.1 %collective-permute-start.22 = (f32[40,128]{1,0:T(8,128)S(1)}, f32[40,128]{1,0:T(8,128)S(1)}, u32[]{:S(2)}, u32[]{:S(2)}) collective-permute-start(f32[40,128]{1,0:T(8,128)S(1)} %add_add_fusion.1), channel_id=1, source_target_pairs={{0,8},{4,12},{8,0},{12,4},{16,24},{20,28},{24,16},{28,20},{32,40},... | collective-permute-start | bytes 61448 | tf_op jit(solution)/shard_map/ppermute | solution.py:40
  104.8 5.8 %collective-permute-start.25 = (f32[40,128]{1,0:T(8,128)S(1)}, f32[40,128]{1,0:T(8,128)S(1)}, u32[]{:S(2)}, u32[]{:S(2)}) collective-permute-start(f32[40,128]{1,0:T(8,128)S(1)} %add.88), channel_id=1, source_target_pairs={{0,48},{4,52},{8,56},{12,60},{16,0},{20,4},{24,8},{28,12},{32,16},... | collective-permute-start | bytes 61448 | tf_op jit(solution)/shard_map/ppermute | solution.py:36
  108.4 4.7 %collective-permute-start.24 = (f32[40,128]{1,0:T(8,128)S(1)}, f32[40,128]{1,0:T(8,128)S(1)}, u32[]{:S(2)}, u32[]{:S(2)}) collective-permute-start(f32[40,128]{1,0:T(8,128)S(1)} %add.88), channel_id=1, source_target_pairs={{0,16},{4,20},{8,24},{12,28},{16,32},{20,36},{24,40},{28,44},{32,4... | collective-permute-start | bytes 61448 | tf_op jit(solution)/shard_map/ppermute | solution.py:36
  108.4 6.5 %collective-permute-start.23 = (f32[40,128]{1,0:T(8,128)S(1)}, f32[40,128]{1,0:T(8,128)S(1)}, u32[]{:S(2)}, u32[]{:S(2)}) collective-permute-start(f32[40,128]{1,0:T(8,128)S(1)} %add.88), channel_id=1, source_target_pairs={{0,32},{4,36},{8,40},{12,44},{16,48},{20,52},{24,56},{28,60},{32,0... | collective-permute-start | bytes 61448 | tf_op jit(solution)/shard_map/ppermute | solution.py:36
  114.9 5.6 %copy-start.2 = (f32[40,128]{1,0:T(8,128)}, f32[40,128]{1,0:T(8,128)S(1)}, u32[]{:S(2)}) copy-start(f32[40,128]{1,0:T(8,128)S(1)} %add_add_fusion.mine) | copy-start | bytes 61444
  114.9 5.6 %collective-permute-start.26 = (f32[40,128]{1,0:T(8,128)S(1)}, f32[40,128]{1,0:T(8,128)S(1)}, u32[]{:S(2)}, u32[]{:S(2)}) collective-permute-start(f32[40,128]{1,0:T(8,128)S(1)} %add_add_fusion.mine), channel_id=1, source_target_pairs={{0,4},{4,0},{8,12},{12,8},{16,20},{20,16},{24,28},{28,24},{32,36},... | collective-permute-start | bytes 61448 | tf_op jit(solution)/shard_map/ppermute | solution.py:28
  120.5 0.6 copy-start.3

commit v2 on v1

v2 whole, which is shorter than its diff:
```python
import functools

import jax
import jax.numpy as jnp
from jax import lax
from jax.experimental import pallas as pl
from jax.experimental.pallas import tpu as pltpu
from jax.sharding import PartitionSpec as P

BW = 128
NTASK = 3
NBIN = 64
NX, NZ, NC, NY = 4, 8, 2, 4
HALF = NBIN // NC
ROWS_B = 16


def coord_pairs(target):
    place = lambda x, z, c: (x * NZ + z) * NC + c
    return [
        (place(x, z, c), place(*target(x, z, c)))
        for x in range(NX)
        for z in range(NZ)
        for c in range(NC)
    ]


def to_core(a):
    return lax.ppermute(a, "coord", coord_pairs(lambda x, z, c: (x, z, 1 - c)))


def along_x(a, d):
    return lax.ppermute(a, "coord", coord_pairs(lambda x, z, c: ((x + d) % NX, z, c)))


def along_z(a, d):
    return lax.ppermute(a, "coord", coord_pairs(lambda x, z, c: (x, (z + d) % NZ, c)))


def z_partner(a):
    return lax.ppermute(a, "coord", coord_pairs(lambda x, z, c: (x, z ^ 1, c)))


def along_y(a, d):
    return lax.ppermute(a, "dp", [(y, (y + d) % NY) for y in range(NY)])


def place_of_device():
    i = lax.axis_index("coord")
    return i // (NZ * NC), (i // NC) % NZ, i % NC


def feature_kernel(cfg, bins_hbm, h_t, g_t, h_v, g_v, proj, out_a, out_b, h_buf, g_buf, hv_buf, gv_buf, p_buf, grads, bins, sem_t, sem_v, sem_p, sem_b):
    layers, n_t, n_v, cols, blk, slots, unroll = cfg
    n = n_t + n_v
    n_a = out_a.shape[1]
    nblk = n_t // blk
    share = cols // nblk

    def train_copies(t):
        l, s = t // nblk, pl.ds((t % nblk) * blk, blk)
        at = t % slots
        return (
            pltpu.make_async_copy(h_t.at[l, s], h_buf.at[at], sem_t.at[0, at]),
            pltpu.make_async_copy(g_t.at[l, s], g_buf.at[at], sem_t.at[1, at]),
        )

    def val_copies(l):
        return (
            pltpu.make_async_copy(h_v.at[l], hv_buf.at[l], sem_v.at[0, l]),
            pltpu.make_async_copy(g_v.at[l], gv_buf.at[l], sem_v.at[1, l]),
        )

    def proj_copy(l):
        return pltpu.make_async_copy(proj.at[l], p_buf.at[l], sem_p.at[l])

    def start(copies):
        for copy in copies:
            copy.start()

    def wait(copies):
        for copy in copies:
            copy.wait()

    bins_copy = pltpu.make_async_copy(bins_hbm, bins, sem_b)
    bins_copy.start()
    for t in range(slots):
        start(train_copies(t))
        if t == 1:
            start(val_copies(0))
    proj_copy(0).start()

    @pl.loop(0, NBIN)
    def _(b):
        out_a[b] = jnp.zeros(out_a.shape[1:], jnp.float32)
        out_b[b] = jnp.zeros(out_b.shape[1:], jnp.float32)

    bins_copy.wait()
    my_x, my_z, my_c = place_of_device()

    def example(l, g, h, e):
        grads[l, pl.ds(e, cols, stride=n), :] = jnp.dot(g, h, preferred_element_type=jnp.float32)

    def project(l, j):
        a = grads[l, pl.ds(j * n, n), :].astype(jnp.bfloat16)
        p = jnp.dot(a, p_buf[l, j], preferred_element_type=jnp.float32)
        b = bins[l, j]
        far_c = (b // HALF) ^ my_c
        far_odd = (b ^ my_z) & 1
        far_quad = ((b - (my_z ^ far_odd)) & (NZ - 1)) // 2
        far_x = ((b // NZ) - my_x) & (NX - 1)
        slot_a = ((far_x + 2) & (NX - 1)) * NZ + far_odd * (NZ // 2) + far_quad
        slot_b = far_odd * (HALF // 2) + far_quad * NX + far_x
        out_a[far_c * HALF + slot_a] += p[:n_a]
        out_b[far_c * HALF + slot_b] += p[n_a:]

    for l in range(layers):

        @pl.loop(0, nblk)
        def _(b):
            t = l * nblk + b
            wait(train_copies(t))
            at = t % slots
            for i in range(blk):
                example(l, g_buf[at, i], h_buf[at, i], b * blk + i)
            if l > 0:
                for i in range(share):
                    project(l - 1, b * share + i)

            @pl.when(t + slots < layers * nblk)
            def _():
                start(train_copies(t + slots))

            if l + 1 < layers:

                @pl.when(b == nblk // 2)
                def _():
                    start(val_copies(l + 1))
                    proj_copy(l + 1).start()

        wait(val_copies(l))
        for i in range(n_v):
            example(l, gv_buf[l, i], hv_buf[l, i], n_t + i)
        proj_copy(l).wait()

    @pl.loop(0, cols, unroll=unroll)
    def _(j):
        project(layers - 1, j)


def local_features(bins, h_t, g_t, h_v, g_v, proj, n_a):
    layers, n_t, tok, r = h_t.shape
    n_v, cols = h_v.shape[1], g_t.shape[2]
    n = n_t + n_v
    blk, slots, unroll = 16, 6, 20
    in_hbm = pl.BlockSpec(memory_space=pltpu.HBM)
    return pl.pallas_call(
        functools.partial(feature_kernel, (layers, n_t, n_v, cols, blk, slots, unroll)),
        out_shape=(
            pltpu.VMEM((NBIN, n_a, BW), jnp.float32),
            pltpu.VMEM((NBIN, n - n_a, BW), jnp.float32),
        ),
        in_specs=[in_hbm] * 6,
        out_specs=[pl.BlockSpec(memory_space=pltpu.VMEM)] * 2,
        scratch_shapes=[
            pltpu.VMEM((slots, blk, tok, r), jnp.bfloat16),
            pltpu.VMEM((slots, blk, cols, tok), jnp.bfloat16),
            pltpu.VMEM((layers, n_v, tok, r), jnp.bfloat16),
            pltpu.VMEM((layers, n_v, cols, tok), jnp.bfloat16),
            pltpu.VMEM((layers, cols, r, BW), jnp.bfloat16),
            pltpu.VMEM((layers, cols * n, r), jnp.float32),
            pltpu.SMEM((layers, cols), jnp.int32),
            pltpu.SemaphoreType.DMA((2, slots)),
            pltpu.SemaphoreType.DMA((2, layers)),
            pltpu.SemaphoreType.DMA((layers,)),
            pltpu.SemaphoreType.DMA,
        ],
        compiler_params=pltpu.CompilerParams(vmem_limit_bytes=42 * 1024 * 1024),
        name="features",
    )(*[pltpu.with_memory_space_constraint(a, pltpu.HBM) for a in (bins, h_t, g_t, h_v, g_v, proj)])


def in_vmem(a):
    return pltpu.with_memory_space_constraint(a, pltpu.VMEM)


def add(parts):
    total = parts[0]
    for part in parts[1:]:
        total = total + part
    return total


def along_z_pairs(a):
    return add([a[0]] + [along_z(a[d], 2 * d) for d in (2, 1, 3)])


def reduce_to_owner(f_a, f_b):
    mid = NZ // 2
    first = to_core(f_a[HALF : HALF + NZ])
    first, rest, far_b = lax.optimization_barrier((first, f_a[HALF + NZ :], f_b[HALF:]))
    far_b, rest = to_core(far_b), to_core(rest)
    half = f_a[:NZ] + first
    right, left = along_x(half[:mid], 1), along_x(half[mid:], -1)
    b = f_b[:HALF] + far_b
    far_b = z_partner(b[HALF // 2 :])
    right, left, rest = lax.optimization_barrier((right, left, rest))
    half = f_a[NZ:HALF] + rest
    right = along_x(jnp.concatenate([half[2 * NZ : 2 * NZ + mid] + right, half[2 * NZ + mid :]]), 1)
    left = along_x(jnp.concatenate([half[:mid], half[mid:NZ] + left]), -1)
    b = (b[: HALF // 2] + far_b).reshape(mid, NX, *b.shape[1:])
    b = along_z_pairs(b)
    a = half[NZ : 2 * NZ] + right + left
    a = a[:mid] + z_partner(a[mid:])
    b = add([b[0]] + [along_x(b[d], d) for d in (2, 1, 3)])
    return along_z_pairs(a), b


def dots_kernel(n_v, rows_a, rows_b, v1, v2, v3, keep, send, val, dots, stats):
    y = lax.axis_index("dp")
    _, _, c = place_of_device()
    n_b = rows_b.shape[0]
    train = rows_a[...]
    if n_b > n_v:
        train = jnp.concatenate([train, rows_b[0 : n_b - n_v, :]])
    val[pl.ds(pl.multiple_of(y * n_v, n_v), n_v), :] = rows_b[n_b - n_v : n_b, :]
    for d, part in ((1, v1), (2, v2), (3, v3)):
        val[pl.ds(pl.multiple_of(((y - d) & (NY - 1)) * n_v, n_v), n_v), :] = part[...]
    v = val[...]
    contract = lambda a, b: lax.dot_general(
        a, b, (((1,), (1,)), ((), ())), precision=lax.Precision.HIGHEST, preferred_element_type=jnp.float32
    )
    dots[...] = contract(v, train)
    ones = jnp.ones((8, BW), jnp.float32)
    stats[0] = contract(ones, train * train)
    stats[1] = jnp.zeros_like(stats[1])
    stats[1, :, 0 : NY * n_v] = contract(ones, v * v)
    rows = NY * n_v // NC
    for ref, h in ((keep, c), (send, 1 - c)):
        ref[0:rows, :] = dots[pl.ds(pl.multiple_of(h * rows, rows), rows), :]
        ref[rows : rows + 8, :] = stats[h]


def scores_kernel(mine, other, tasks, cos_out, score_out, dots, stats):
    _, _, c = place_of_device()
    n_v = tasks.shape[1]
    rows = n_v // NC
    for ref, h in ((mine, c), (other, 1 - c)):
        dots[pl.ds(pl.multiple_of(h * rows, rows), rows), :] = ref[0:rows, :]
        stats[h] = ref[rows : rows + 8, :]
    on_diagonal = lax.broadcasted_iota(jnp.int32, (n_v, n_v), 0) == lax.broadcasted_iota(jnp.int32, (n_v, n_v), 1)
    train_norm = jnp.sqrt(stats[0, 0:1, :] + 1e-06)
    val_norm_row = jnp.sqrt(stats[1, 0:1, 0:n_v] + 1e-06)
    val_norm = jnp.sum(jnp.where(on_diagonal, val_norm_row, 0.0), axis=1, keepdims=True)
    cos = dots[...] / (train_norm * val_norm)
    cos_out[...] = cos
    task_row = tasks[...].astype(jnp.float32)
    task = jnp.sum(jnp.where(on_diagonal, task_row, 0.0), axis=1, keepdims=True)
    for s in range(NTASK):
        member = (task == float(s)).astype(jnp.float32)
        count = jnp.sum(member, axis=0, keepdims=True)
        score_out[s : s + 1, :] = jnp.sum(cos * member, axis=0, keepdims=True) / count


def per_device(h_train, gout_train, h_val, gout_val, proj, bins, tasks):
    n_t, n_v = h_train.shape[1], h_val.shape[1]
    all_v = n_v * NY
    n_a = n_t - ROWS_B
    f_a, f_b = local_features(
        bins, h_train, jnp.swapaxes(gout_train, 2, 3), h_val, jnp.swapaxes(gout_val, 2, 3), proj, n_a
    )
    rows_a, rows_b = reduce_to_owner(f_a, f_b)
    v = rows_b[ROWS_B:]
    others = [along_y(v, d) for d in (1, 2, 3)]
    part = pltpu.VMEM((all_v // NC + 8, n_t), jnp.float32)
    keep, send = pl.pallas_call(
        functools.partial(dots_kernel, n_v),
        out_shape=(part, part),
        scratch_shapes=[
            pltpu.VMEM((all_v, BW), jnp.float32),
            pltpu.VMEM((all_v, n_t), jnp.float32),
            pltpu.VMEM((NC, 8, n_t), jnp.float32),
        ],
        name="dots",
    )(*map(in_vmem, (rows_a, rows_b, *others)))
    a = keep + to_core(send)
    got = [along_x(a, d) for d in (2, 1, 3)]
    a = a + got[0] + got[1] + got[2]
    a = a + z_partner(a)
    a = add([a] + [along_z(a, d) for d in (4, 2, 6)])
    cos_t, scores_t = pl.pallas_call(
        scores_kernel,
        out_shape=(
            jax.ShapeDtypeStruct((all_v, n_t), jnp.float32),
            jax.ShapeDtypeStruct((NTASK, n_t), jnp.float32),
        ),
        scratch_shapes=[
            pltpu.VMEM((all_v, n_t), jnp.float32),
            pltpu.VMEM((NC, 8, n_t), jnp.float32),
        ],
        name="scores",
    )(in_vmem(a), in_vmem(to_core(a)), tasks.reshape(1, all_v))
    return cos_t.T, scores_t.T


def solution(mesh):
    in_specs = (
        P(None, "dp", None, None),
        P(None, "dp", None, "coord"),
        P(None, "dp", None, None),
        P(None, "dp", None, "coord"),
        P(None, "coord", None, None),
        P(None, "coord"),
        P(),
    )
    out_specs = (P("dp", None), P("dp", None))
    return jax.shard_map(
        per_device, mesh=mesh, in_specs=in_specs, out_specs=out_specs, check_vma=False
    )
```

time: 123 us -> 96.6 us (0.79)
  waiting for transfers between devices: 44.4 us -> 23.6 us
  Pallas kernels: 25.1 us -> 17.9 us
  starting transfers between devices: 47.3 us -> 53.3 us
  local copies, waits for them, and re-layouts: 3.69 us -> 0.26 us
    ppermute x7 -> x10, waiting for transfers between devices: 25.6 us -> 9.61 us  [along_x(): lax.ppermute(a, 'coord', coord_pairs(lambda x, z, c: ((x + d) % NX, z, c)))]
    ppermute x10 -> x9, waiting for transfers between devices: 9.92 us -> 3.86 us  [along_z(): lax.ppermute(a, 'coord', coord_pairs(lambda x, z, c: (x, (z + d) % NZ, c)))]
    pallas_call x1, Pallas kernels: 21.7 us -> 16.1 us  [local_features(): pl.pallas_call(functools.partial(feature_kernel, (layers, n_t, n_v, cols,...]
    ppermute x7 -> x10, starting transfers between devices: 5.91 us -> 10.2 us  [along_x(): lax.ppermute(a, 'coord', coord_pairs(lambda x, z, c: ((x + d) % NX, z, c)))]
    unnamed x14 -> x0, local copies, waits for them, and re-layouts: 1.71 us -> none
    slice x3 -> x8, local copies, waits for them, and re-layouts: 1.95 us -> 0.24 us  [the longest x1 0.09 us: reduce_to_owner(): f_a[HALF + NZ:]]
    pallas_call x1, Pallas kernels: 1.9 us -> 0.37 us  [per_device(): pl.pallas_call(functools.partial(dots_kernel, n_v), out_shape=(part, part...]
    ppermute x1 -> x3, starting transfers between devices: 1.97 us -> 2.96 us  [z_partner(): return lax.ppermute(a, 'coord', coord_pairs(lambda x, z, c: (x, z ^ 1, c)))]
  transfers between devices with their start and end apart: 27 -> 30, of which waited for: 20 -> 18; matrix products, arithmetic and copies ran while one was open for 0% -> 1% of each run, Pallas kernels for 0% -> 0%
where the time goes in v2:
time: 96.6 us
  starting transfers between devices  53.3 us (55%)
  waiting for transfers between devices  23.6 us (24%)
  Pallas kernels  17.9 us (19%)
    ppermute x9, starting transfers between devices, along_z(): lax.ppermute(a, 'coord', coord_pairs(lambda x, z, c: (x, (z + d) % NZ, c)))  21.7 us
    pallas_call x1, Pallas kernels, local_features(): pl.pallas_call(functools.partial(feature_kernel, (layers, n_t, n_v, cols,...  16.1 us
    ppermute x5, starting transfers between devices, to_core(): return lax.ppermute(a, 'coord', coord_pairs(lambda x, z, c: (x, z, 1 - c)))  14.5 us
    ppermute x10, starting transfers between devices, along_x(): lax.ppermute(a, 'coord', coord_pairs(lambda x, z, c: ((x + d) % NX, z, c)))  10.2 us
    ppermute x10, waiting for transfers between devices, along_x(): lax.ppermute(a, 'coord', coord_pairs(lambda x, z, c: ((x + d) % NX, z, c)))  9.61 us
    ppermute x5, waiting for transfers between devices, to_core(): return lax.ppermute(a, 'coord', coord_pairs(lambda x, z, c: (x, z, 1 - c)))  4.73 us
    ppermute x9, waiting for transfers between devices, along_z(): lax.ppermute(a, 'coord', coord_pairs(lambda x, z, c: (x, (z + d) % NZ, c)))  3.86 us
    ppermute x3, starting transfers between devices, along_y(): return lax.ppermute(a, 'dp', [(y, (y + d) % NY) for y in range(NY)])  3.85 us
  transfers between devices with their start and end apart: 30, of which 18 were waited for; matrix products, arithmetic and copies ran while one was open for 1% of the time, Pallas kernels for 0%

profile of v2, /device:TPU:1, one launch (start us, length us, event | category | flops | bytes accessed | tf_op | source)
XLA Modules:
  0.0 96.6 jit_solution(2444756029683301926)
XLA Ops:
  0.6 16.1 %features.1 = (f32[64,112,128]{2,1,0:T(8,128)S(1)}, f32[64,32,128]{2,1,0:T(8,128)S(1)}) custom-call(s32[2,80]{1,0:T(2,128)} %bins_hbm.1, bf16[2,128,256,128]{3,2,1,0:T(8,128)(2,1)} %h_t.1, bf16[2,128,80,256]{3,2,1,0:T(8,128)(2,1)} %bitcast.33, bf16[2,16,256,128]{3,2,1,0:T(8,128)(2,1)} %h_v.1, bf16[2,16,80,256]{3,2,1,0:T(8,128)(2,1)} %bitcast.34, ...), custom_call_target="tpu_custom_call" | custom-call | tf_op jit(solution)/shard_map/features/pallas_call | solution.py:157
  16.8 3.3 %collective-permute-start = (f32[8,112,128]{2,1,0:T(8,128)S(1)}, f32[8,112,128]{2,1,0:T(8,128)S(1)}, u32[]{:S(2)}, u32[]{:S(2)}) collective-permute-start(f32[8,112,128]{2,1,0:T(8,128)S(1)} %slice.96), channel_id=1, source_target_pairs={{0,4},{4,0},{8,12},{12,8},{16,20},{20,16},{24,28},{28,24},{32,36},... | collective-permute-start | bytes 1376264 | tf_op jit(solution)/shard_map/ppermute | solution.py:29
  20.1 0.1 slice.97
  20.3 1.3 %collective-permute-done = f32[8,112,128]{2,1,0:T(8,128)S(1)} collective-permute-done((f32[8,112,128]{2,1,0:T(8,128)S(1)}, f32[8,112,128]{2,1,0:T(8,128)S(1)}, u32[]{:S(2)}, u32[]{:S(2)}) %collective-permute-start) | collective-permute-done | bytes 458784 | tf_op jit(solution)/shard_map/ppermute | solution.py:29
  21.6 0.4 collective-permute-start.3
  22.0 0.1 collective-permute-start.10
  22.2 0.8 collective-permute-start.2
  23.0 0.7 collective-permute-start.1
  23.7 1.7 %collective-permute-done.10 = f32[32,32,128]{2,1,0:T(8,128)S(1)} collective-permute-done((f32[32,32,128]{2,1,0:T(8,128)S(1)}, f32[32,32,128]{2,1,0:T(8,128)S(1)}, u32[]{:S(2)}, u32[]{:S(2)}) %collective-permute-start.10) | collective-permute-done | bytes 524320 | tf_op jit(solution)/shard_map/ppermute | solution.py:29
  25.5 0.1 slice_add_fusion.1
  25.6 0.1 collective-permute-start.11
  25.7 3.4 %collective-permute-done.2 = f32[4,112,128]{2,1,0:T(8,128)S(1)} collective-permute-done((f32[4,112,128]{2,1,0:T(8,128)S(1)}, f32[4,112,128]{2,1,0:T(8,128)S(1)}, u32[]{:S(2)}, u32[]{:S(2)}) %collective-permute-start.2) | collective-permute-done | bytes 229408 | tf_op jit(solution)/shard_map/ppermute | solution.py:33
  29.1 1.6 %collective-permute-done.1 = f32[4,112,128]{2,1,0:T(8,128)S(1)} collective-permute-done((f32[4,112,128]{2,1,0:T(8,128)S(1)}, f32[4,112,128]{2,1,0:T(8,128)S(1)}, u32[]{:S(2)}, u32[]{:S(2)}) %collective-permute-start.1) | collective-permute-done | bytes 229408 | tf_op jit(solution)/shard_map/ppermute | solution.py:33
  30.7 0.0 collective-permute-done.3
  30.7 0.2 slice_add_fusion
  30.9 0.1 slice_add_fusion.7
  31.0 0.4 collective-permute-start.5
  31.5 1.2 %collective-permute-start.4 = (f32[8,112,128]{2,1,0:T(8,128)S(1)}, f32[8,112,128]{2,1,0:T(8,128)S(1)}, u32[]{:S(2)}, u32[]{:S(2)}) collective-permute-start(f32[8,112,128]{2,1,0:T(8,128)S(1)} %pad_maximum_fusion), channel_id=1, source_target_pairs={{0,64},{4,68},{8,72},{12,76},{16,80},{20,84},{24,88},{28,92},{32,9... | collective-permute-start | bytes 1376264 | tf_op jit(solution)/shard_map/ppermute | solution.py:33
  32.7 0.5 collective-permute-done.11
  33.3 6.5 %collective-permute-start.12 = (f32[4,32,128]{2,1,0:T(8,128)S(1)}, f32[4,32,128]{2,1,0:T(8,128)S(1)}, u32[]{:S(2)}, u32[]{:S(2)}) collective-permute-start(f32[4,32,128]{2,1,0:T(8,128)S(1)} %get-tuple-element.32), channel_id=1, source_target_pairs={{0,32},{4,36},{8,40},{12,44},{16,48},{20,52},{24,56},{28,60},{32,0... | collective-permute-start | bytes 196616 | tf_op jit(solution)/shard_map/ppermute | solution.py:37
  39.8 0.0 collective-permute-start.14
  39.8 2.4 %collective-permute-start.13 = (f32[4,32,128]{2,1,0:T(8,128)S(1)}, f32[4,32,128]{2,1,0:T(8,128)S(1)}, u32[]{:S(2)}, u32[]{:S(2)}) collective-permute-start(f32[4,32,128]{2,1,0:T(8,128)S(1)} %get-tuple-element.34), channel_id=1, source_target_pairs={{0,16},{4,20},{8,24},{12,28},{16,32},{20,36},{24,40},{28,44},{32,4... | collective-permute-start | bytes 196616 | tf_op jit(solution)/shard_map/ppermute | solution.py:37
  42.1 0.0 collective-permute-done.5
  42.1 1.2 %collective-permute-done.4 = f32[8,112,128]{2,1,0:T(8,128)S(1)} collective-permute-done((f32[8,112,128]{2,1,0:T(8,128)S(1)}, f32[8,112,128]{2,1,0:T(8,128)S(1)}, u32[]{:S(2)}, u32[]{:S(2)}) %collective-permute-start.4) | collective-permute-done | bytes 458784 | tf_op jit(solution)/shard_map/ppermute | solution.py:33
  43.3 0.1 fusion
  43.4 1.7 %collective-permute-start.6 = (f32[4,112,128]{2,1,0:T(8,128)S(1)}, f32[4,112,128]{2,1,0:T(8,128)S(1)}, u32[]{:S(2)}, u32[]{:S(2)}) collective-permute-start(f32[4,112,128]{2,1,0:T(8,128)S(1)} %slice.132), channel_id=1, source_target_pairs={{0,8},{4,12},{8,0},{12,4},{16,24},{20,28},{24,16},{28,20},{32,40},... | collective-permute-start | bytes 688136 | tf_op jit(solution)/shard_map/ppermute | solution.py:41
  45.1 0.5 collective-permute-done.14
  45.6 0.0 collective-permute-done.13
  45.7 3.4 %collective-permute-start.15 = (f32[32,128]{1,0:T(8,128)S(1)}, f32[32,128]{1,0:T(8,128)S(1)}, u32[]{:S(2)}, u32[]{:S(2)}) collective-permute-start(f32[32,128]{1,0:T(8,128)S(1)} %get-tuple-element.38), channel_id=1, source_target_pairs={{0,128},{4,132},{8,136},{12,140},{16,144},{20,148},{24,152},{28,15... | collective-permute-start | bytes 49160 | tf_op jit(solution)/shard_map/ppermute | solution.py:33
  49.1 0.0 collective-permute-start.17
  49.1 1.5 %collective-permute-start.16 = (f32[32,128]{1,0:T(8,128)S(1)}, f32[32,128]{1,0:T(8,128)S(1)}, u32[]{:S(2)}, u32[]{:S(2)}) collective-permute-start(f32[32,128]{1,0:T(8,128)S(1)} %get-tuple-element.40), channel_id=1, source_target_pairs={{0,64},{4,68},{8,72},{12,76},{16,80},{20,84},{24,88},{28,92},{32,9... | collective-permute-start | bytes 49160 | tf_op jit(solution)/shard_map/ppermute | solution.py:33
  50.5 0.1 collective-permute-done.6
  50.7 4.8 %collective-permute-start.7 = (f32[112,128]{1,0:T(8,128)S(1)}, f32[112,128]{1,0:T(8,128)S(1)}, u32[]{:S(2)}, u32[]{:S(2)}) collective-permute-start(f32[112,128]{1,0:T(8,128)S(1)} %get-tuple-element.35), channel_id=1, source_target_pairs={{0,32},{4,36},{8,40},{12,44},{16,48},{20,52},{24,56},{28,60},{32,0... | collective-permute-start | bytes 172040 | tf_op jit(solution)/shard_map/ppermute | solution.py:37
  55.4 0.0 collective-permute-start.9
  55.4 0.0 collective-permute-done.15
  55.4 2.4 %collective-permute-start.8 = (f32[112,128]{1,0:T(8,128)S(1)}, f32[112,128]{1,0:T(8,128)S(1)}, u32[]{:S(2)}, u32[]{:S(2)}) collective-permute-start(f32[112,128]{1,0:T(8,128)S(1)} %get-tuple-element.37), channel_id=1, source_target_pairs={{0,16},{4,20},{8,24},{12,28},{16,32},{20,36},{24,40},{28,44},{32,4... | collective-permute-start | bytes 172040 | tf_op jit(solution)/shard_map/ppermute | solution.py:37
  57.8 2.8 %collective-permute-start.20 = (f32[16,128]{1,0:T(8,128)S(1)}, f32[16,128]{1,0:T(8,128)S(1)}, u32[]{:S(2)}, u32[]{:S(2)}) collective-permute-start(f32[16,128]{1,0:T(8,128)S(1)} %slice.147), channel_id=1, source_target_pairs={{0,3},{1,0},{2,1},{3,2},{4,7},{5,4},{6,5},{7,6},{8,11},{9,8},{10,9... | collective-permute-start | bytes 24584 | tf_op jit(solution)/shard_map/ppermute | solution.py:45
  60.6 0.3 collective-permute-start.19
  61.0 0.0 collective-permute-done.7
  61.0 0.7 collective-permute-start.18
  61.7 0.0 collective-permute-done.9
  61.7 0.0 collective-permute-done.8
  61.8 3.2 %collective-permute-done.19.v2 = f32[16,128]{1,0:T(8,128)S(1)} collective-permute-done((f32[16,128]{1,0:T(8,128)S(1)}, f32[16,128]{1,0:T(8,128)S(1)}, u32[]{:S(2)}, u32[]{:S(2)}) %collective-permute-start.19) | collective-permute-done | bytes 8224 | tf_op jit(solution)/shard_map/ppermute | solution.py:45
  64.9 0.1 collective-permute-done.18.v1
  65.0 0.4 dots.1
  65.4 5.8 %collective-permute-start.21 = (f32[40,128]{1,0:T(8,128)S(1)}, f32[40,128]{1,0:T(8,128)S(1)}, u32[]{:S(2)}, u32[]{:S(2)}) collective-permute-start(f32[40,128]{1,0:T(8,128)S(1)} %get-tuple-element.23), channel_id=1, source_target_pairs={{0,4},{4,0},{8,12},{12,8},{16,20},{20,16},{24,28},{28,24},{32,36},... | collective-permute-start | bytes 61448 | tf_op jit(solution)/shard_map/ppermute | solution.py:29
  71.2 0.8 collective-permute-done.21
  72.1 1.0 %collective-permute-start.24 = (f32[40,128]{1,0:T(8,128)S(1)}, f32[40,128]{1,0:T(8,128)S(1)}, u32[]{:S(2)}, u32[]{:S(2)}) collective-permute-start(f32[40,128]{1,0:T(8,128)S(1)} %add.96), channel_id=1, source_target_pairs={{0,192},{4,196},{8,200},{12,204},{16,208},{20,212},{24,216},{28,22... | collective-permute-start | bytes 61448 | tf_op jit(solution)/shard_map/ppermute | solution.py:33
  73.0 0.5 collective-permute-start.23
  73.5 0.7 collective-permute-start.22
  74.3 0.4 collective-permute-done.24
  74.7 2.2 %collective-permute-done.23 = f32[40,128]{1,0:T(8,128)S(1)} collective-permute-done((f32[40,128]{1,0:T(8,128)S(1)}, f32[40,128]{1,0:T(8,128)S(1)}, u32[]{:S(2)}, u32[]{:S(2)}) %collective-permute-start.23) | collective-permute-done | bytes 20512 | tf_op jit(solution)/shard_map/ppermute | solution.py:33
  76.9 0.8 collective-permute-done.22
  77.7 1.1 %collective-permute-start.25 = (f32[40,128]{1,0:T(8,128)S(1)}, f32[40,128]{1,0:T(8,128)S(1)}, u32[]{:S(2)}, u32[]{:S(2)}) collective-permute-start(f32[40,128]{1,0:T(8,128)S(1)} %add_add_fusion.1), channel_id=1, source_target_pairs={{0,8},{4,12},{8,0},{12,4},{16,24},{20,28},{24,16},{28,20},{32,40},... | collective-permute-start | bytes 61448 | tf_op jit(solution)/shard_map/ppermute | solution.py:41
  78.8 1.6 %collective-permute-done.25 = f32[40,128]{1,0:T(8,128)S(1)} collective-permute-done((f32[40,128]{1,0:T(8,128)S(1)}, f32[40,128]{1,0:T(8,128)S(1)}, u32[]{:S(2)}, u32[]{:S(2)}) %collective-permute-start.25) | collective-permute-done | bytes 20512 | tf_op jit(solution)/shard_map/ppermute | solution.py:41
  80.4 1.0 %collective-permute-start.28 = (f32[40,128]{1,0:T(8,128)S(1)}, f32[40,128]{1,0:T(8,128)S(1)}, u32[]{:S(2)}, u32[]{:S(2)}) collective-permute-start(f32[40,128]{1,0:T(8,128)S(1)} %add.100), channel_id=1, source_target_pairs={{0,48},{4,52},{8,56},{12,60},{16,0},{20,4},{24,8},{28,12},{32,16},... | collective-permute-start | bytes 61448 | tf_op jit(solution)/shard_map/ppermute | solution.py:37
  81.4 1.5 %collective-permute-start.27 = (f32[40,128]{1,0:T(8,128)S(1)}, f32[40,128]{1,0:T(8,128)S(1)}, u32[]{:S(2)}, u32[]{:S(2)}) collective-permute-start(f32[40,128]{1,0:T(8,128)S(1)} %add.100), channel_id=1, source_target_pairs={{0,16},{4,20},{8,24},{12,28},{16,32},{20,36},{24,40},{28,44},{32,4... | collective-permute-start | bytes 61448 | tf_op jit(solution)/shard_map/ppermute | solution.py:37
  82.9 3.2 %collective-permute-start.26 = (f32[40,128]{1,0:T(8,128)S(1)}, f32[40,128]{1,0:T(8,128)S(1)}, u32[]{:S(2)}, u32[]{:S(2)}) collective-permute-start(f32[40,128]{1,0:T(8,128)S(1)} %add.100), channel_id=1, source_target_pairs={{0,32},{4,36},{8,40},{12,44},{16,48},{20,52},{24,56},{28,60},{32,0... | collective-permute-start | bytes 61448 | tf_op jit(solution)/shard_map/ppermute | solution.py:37
  86.1 0.0 collective-permute-done.28
  86.1 0.1 collective-permute-done.27
  86.2 3.3 %collective-permute-done.26 = f32[40,128]{1,0:T(8,128)S(1)} collective-permute-done((f32[40,128]{1,0:T(8,128)S(1)}, f32[40,128]{1,0:T(8,128)S(1)}, u32[]{:S(2)}, u32[]{:S(2)}) %collective-permute-start.26) | collective-permute-done | bytes 20512 | tf_op jit(solution)/shard_map/ppermute | solution.py:37
  89.4 4.9 %collective-permute-start.29 = (f32[40,128]{1,0:T(8,128)S(1)}, f32[40,128]{1,0:T(8,128)S(1)}, u32[]{:S(2)}, u32[]{:S(2)}) collective-permute-start(f32[40,128]{1,0:T(8,128)S(1)} %add_add_fusion.mine), channel_id=1, source_target_pairs={{0,4},{4,0},{8,12},{12,8},{16,20},{20,16},{24,28},{28,24},{32,36},... | collective-permute-start | bytes 61448 | tf_op jit(solution)/shard_map/ppermute | solution.py:29
  94.3 0.8 collective-permute-done.29.other
  95.2 1.4 %scores.1 = (f32[64,128]{1,0:T(8,128)}, f32[3,128]{1,0:T(4,128)}) custom-call(f32[40,128]{1,0:T(8,128)S(1)} %add_add_fusion.mine, f32[40,128]{1,0:T(8,128)S(1)} %collective-permute-done.29.other, s32[1,64]{1,0:T(1,128)} %bitcast.35), custom_call_target="tpu_custom_call" | custom-call | tf_op jit(solution)/shard_map/scores/pallas_call | solution.py:291
  (25 shorter events, 0.4 us)
Async XLA Ops:
  16.8 4.8 %collective-permute-start = (f32[8,112,128]{2,1,0:T(8,128)S(1)}, f32[8,112,128]{2,1,0:T(8,128)S(1)}, u32[]{:S(2)}, u32[]{:S(2)}) collective-permute-start(f32[8,112,128]{2,1,0:T(8,128)S(1)} %slice.96), channel_id=1, source_target_pairs={{0,4},{4,0},{8,12},{12,8},{16,20},{20,16},{24,28},{28,24},{32,36},... | collective-permute-start | bytes 1376264 | tf_op jit(solution)/shard_map/ppermute | solution.py:29
  21.6 9.1 %collective-permute-start.3 = (f32[24,112,128]{2,1,0:T(8,128)S(1)}, f32[24,112,128]{2,1,0:T(8,128)S(1)}, u32[]{:S(2)}, u32[]{:S(2)}) collective-permute-start(f32[24,112,128]{2,1,0:T(8,128)S(1)} %slice.97), channel_id=1, source_target_pairs={{0,4},{4,0},{8,12},{12,8},{16,20},{20,16},{24,28},{28,24},{32,36},... | collective-permute-start | bytes 4128776 | tf_op jit(solution)/shard_map/ppermute | solution.py:29
  22.0 3.5 %collective-permute-start.10 = (f32[32,32,128]{2,1,0:T(8,128)S(1)}, f32[32,32,128]{2,1,0:T(8,128)S(1)}, u32[]{:S(2)}, u32[]{:S(2)}) collective-permute-start(f32[32,32,128]{2,1,0:T(8,128)S(1)} %slice.98), channel_id=1, source_target_pairs={{0,4},{4,0},{8,12},{12,8},{16,20},{20,16},{24,28},{28,24},{32,36},... | collective-permute-start | bytes 1572872 | tf_op jit(solution)/shard_map/ppermute | solution.py:29
  22.2 6.9 %collective-permute-start.2 = (f32[4,112,128]{2,1,0:T(8,128)S(1)}, f32[4,112,128]{2,1,0:T(8,128)S(1)}, u32[]{:S(2)}, u32[]{:S(2)}) collective-permute-start(f32[4,112,128]{2,1,0:T(8,128)S(1)} %get-tuple-element.30), channel_id=1, source_target_pairs={{0,192},{4,196},{8,200},{12,204},{16,208},{20,212},{24,216},{28,22... | collective-permute-start | bytes 688136 | tf_op jit(solution)/shard_map/ppermute | solution.py:33
  23.0 7.7 %collective-permute-start.1 = (f32[4,112,128]{2,1,0:T(8,128)S(1)}, f32[4,112,128]{2,1,0:T(8,128)S(1)}, u32[]{:S(2)}, u32[]{:S(2)}) collective-permute-start(f32[4,112,128]{2,1,0:T(8,128)S(1)} %get-tuple-element.31), channel_id=1, source_target_pairs={{0,64},{4,68},{8,72},{12,76},{16,80},{20,84},{24,88},{28,92},{32,9... | collective-permute-start | bytes 688136 | tf_op jit(solution)/shard_map/ppermute | solution.py:33
  25.6 7.6 %collective-permute-start.11 = (f32[16,32,128]{2,1,0:T(8,128)S(1)}, f32[16,32,128]{2,1,0:T(8,128)S(1)}, u32[]{:S(2)}, u32[]{:S(2)}) collective-permute-start(f32[16,32,128]{2,1,0:T(8,128)S(1)} %slice.138), channel_id=1, source_target_pairs={{0,8},{4,12},{8,0},{12,4},{16,24},{20,28},{24,16},{28,20},{32,40},... | collective-permute-start | bytes 786440 | tf_op jit(solution)/shard_map/ppermute | solution.py:41
  31.0 11.1 %collective-permute-start.5 = (f32[8,112,128]{2,1,0:T(8,128)S(1)}, f32[8,112,128]{2,1,0:T(8,128)S(1)}, u32[]{:S(2)}, u32[]{:S(2)}) collective-permute-start(f32[8,112,128]{2,1,0:T(8,128)S(1)} %pad_maximum_fusion.1), channel_id=1, source_target_pairs={{0,192},{4,196},{8,200},{12,204},{16,208},{20,212},{24,216},{28,22... | collective-permute-start | bytes 1376264 | tf_op jit(solution)/shard_map/ppermute | solution.py:33
  31.5 11.8 %collective-permute-start.4 = (f32[8,112,128]{2,1,0:T(8,128)S(1)}, f32[8,112,128]{2,1,0:T(8,128)S(1)}, u32[]{:S(2)}, u32[]{:S(2)}) collective-permute-start(f32[8,112,128]{2,1,0:T(8,128)S(1)} %pad_maximum_fusion), channel_id=1, source_target_pairs={{0,64},{4,68},{8,72},{12,76},{16,80},{20,84},{24,88},{28,92},{32,9... | collective-permute-start | bytes 1376264 | tf_op jit(solution)/shard_map/ppermute | solution.py:33
  33.3 11.9 %collective-permute-start.12 = (f32[4,32,128]{2,1,0:T(8,128)S(1)}, f32[4,32,128]{2,1,0:T(8,128)S(1)}, u32[]{:S(2)}, u32[]{:S(2)}) collective-permute-start(f32[4,32,128]{2,1,0:T(8,128)S(1)} %get-tuple-element.32), channel_id=1, source_target_pairs={{0,32},{4,36},{8,40},{12,44},{16,48},{20,52},{24,56},{28,60},{32,0... | collective-permute-start | bytes 196616 | tf_op jit(solution)/shard_map/ppermute | solution.py:37
  39.8 5.9 %collective-permute-start.14 = (f32[4,32,128]{2,1,0:T(8,128)S(1)}, f32[4,32,128]{2,1,0:T(8,128)S(1)}, u32[]{:S(2)}, u32[]{:S(2)}) collective-permute-start(f32[4,32,128]{2,1,0:T(8,128)S(1)} %get-tuple-element.33), channel_id=1, source_target_pairs={{0,48},{4,52},{8,56},{12,60},{16,0},{20,4},{24,8},{28,12},{32,16},... | collective-permute-start | bytes 196616 | tf_op jit(solution)/shard_map/ppermute | solution.py:37
  39.8 5.9 %collective-permute-start.13 = (f32[4,32,128]{2,1,0:T(8,128)S(1)}, f32[4,32,128]{2,1,0:T(8,128)S(1)}, u32[]{:S(2)}, u32[]{:S(2)}) collective-permute-start(f32[4,32,128]{2,1,0:T(8,128)S(1)} %get-tuple-element.34), channel_id=1, source_target_pairs={{0,16},{4,20},{8,24},{12,28},{16,32},{20,36},{24,40},{28,44},{32,4... | collective-permute-start | bytes 196616 | tf_op jit(solution)/shard_map/ppermute | solution.py:37
  43.4 7.2 %collective-permute-start.6 = (f32[4,112,128]{2,1,0:T(8,128)S(1)}, f32[4,112,128]{2,1,0:T(8,128)S(1)}, u32[]{:S(2)}, u32[]{:S(2)}) collective-permute-start(f32[4,112,128]{2,1,0:T(8,128)S(1)} %slice.132), channel_id=1, source_target_pairs={{0,8},{4,12},{8,0},{12,4},{16,24},{20,28},{24,16},{28,20},{32,40},... | collective-permute-start | bytes 688136 | tf_op jit(solution)/shard_map/ppermute | solution.py:41
  45.7 9.8 %collective-permute-start.15 = (f32[32,128]{1,0:T(8,128)S(1)}, f32[32,128]{1,0:T(8,128)S(1)}, u32[]{:S(2)}, u32[]{:S(2)}) collective-permute-start(f32[32,128]{1,0:T(8,128)S(1)} %get-tuple-element.38), channel_id=1, source_target_pairs={{0,128},{4,132},{8,136},{12,140},{16,144},{20,148},{24,152},{28,15... | collective-permute-start | bytes 49160 | tf_op jit(solution)/shard_map/ppermute | solution.py:33
  49.1 8.7 %collective-permute-start.17 = (f32[32,128]{1,0:T(8,128)S(1)}, f32[32,128]{1,0:T(8,128)S(1)}, u32[]{:S(2)}, u32[]{:S(2)}) collective-permute-start(f32[32,128]{1,0:T(8,128)S(1)} %get-tuple-element.39), channel_id=1, source_target_pairs={{0,192},{4,196},{8,200},{12,204},{16,208},{20,212},{24,216},{28,22... | collective-permute-start | bytes 49160 | tf_op jit(solution)/shard_map/ppermute | solution.py:33
  49.1 8.7 %collective-permute-start.16 = (f32[32,128]{1,0:T(8,128)S(1)}, f32[32,128]{1,0:T(8,128)S(1)}, u32[]{:S(2)}, u32[]{:S(2)}) collective-permute-start(f32[32,128]{1,0:T(8,128)S(1)} %get-tuple-element.40), channel_id=1, source_target_pairs={{0,64},{4,68},{8,72},{12,76},{16,80},{20,84},{24,88},{28,92},{32,9... | collective-permute-start | bytes 49160 | tf_op jit(solution)/shard_map/ppermute | solution.py:33
  50.7 10.3 %collective-permute-start.7 = (f32[112,128]{1,0:T(8,128)S(1)}, f32[112,128]{1,0:T(8,128)S(1)}, u32[]{:S(2)}, u32[]{:S(2)}) collective-permute-start(f32[112,128]{1,0:T(8,128)S(1)} %get-tuple-element.35), channel_id=1, source_target_pairs={{0,32},{4,36},{8,40},{12,44},{16,48},{20,52},{24,56},{28,60},{32,0... | collective-permute-start | bytes 172040 | tf_op jit(solution)/shard_map/ppermute | solution.py:37
  55.4 6.3 %collective-permute-start.9 = (f32[112,128]{1,0:T(8,128)S(1)}, f32[112,128]{1,0:T(8,128)S(1)}, u32[]{:S(2)}, u32[]{:S(2)}) collective-permute-start(f32[112,128]{1,0:T(8,128)S(1)} %get-tuple-element.36), channel_id=1, source_target_pairs={{0,48},{4,52},{8,56},{12,60},{16,0},{20,4},{24,8},{28,12},{32,16},... | collective-permute-start | bytes 172040 | tf_op jit(solution)/shard_map/ppermute | solution.py:37
  55.4 6.3 %collective-permute-start.8 = (f32[112,128]{1,0:T(8,128)S(1)}, f32[112,128]{1,0:T(8,128)S(1)}, u32[]{:S(2)}, u32[]{:S(2)}) collective-permute-start(f32[112,128]{1,0:T(8,128)S(1)} %get-tuple-element.37), channel_id=1, source_target_pairs={{0,16},{4,20},{8,24},{12,28},{16,32},{20,36},{24,40},{28,44},{32,4... | collective-permute-start | bytes 172040 | tf_op jit(solution)/shard_map/ppermute | solution.py:37
  57.8 3.9 %collective-permute-start.20 = (f32[16,128]{1,0:T(8,128)S(1)}, f32[16,128]{1,0:T(8,128)S(1)}, u32[]{:S(2)}, u32[]{:S(2)}) collective-permute-start(f32[16,128]{1,0:T(8,128)S(1)} %slice.147), channel_id=1, source_target_pairs={{0,3},{1,0},{2,1},{3,2},{4,7},{5,4},{6,5},{7,6},{8,11},{9,8},{10,9... | collective-permute-start | bytes 24584 | tf_op jit(solution)/shard_map/ppermute | solution.py:45
  60.6 4.3 %collective-permute-start.19 = (f32[16,128]{1,0:T(8,128)S(1)}, f32[16,128]{1,0:T(8,128)S(1)}, u32[]{:S(2)}, u32[]{:S(2)}) collective-permute-start(f32[16,128]{1,0:T(8,128)S(1)} %slice.147), channel_id=1, source_target_pairs={{0,2},{1,3},{2,0},{3,1},{4,6},{5,7},{6,4},{7,5},{8,10},{9,11},{10,... | collective-permute-start | bytes 24584 | tf_op jit(solution)/shard_map/ppermute | solution.py:45
  61.0 4.0 %collective-permute-start.18 = (f32[16,128]{1,0:T(8,128)S(1)}, f32[16,128]{1,0:T(8,128)S(1)}, u32[]{:S(2)}, u32[]{:S(2)}) collective-permute-start(f32[16,128]{1,0:T(8,128)S(1)} %slice.147), channel_id=1, source_target_pairs={{0,1},{1,2},{2,3},{3,0},{4,5},{5,6},{6,7},{7,4},{8,9},{9,10},{10,1... | collective-permute-start | bytes 24584 | tf_op jit(solution)/shard_map/ppermute | solution.py:45
  65.4 6.6 %collective-permute-start.21 = (f32[40,128]{1,0:T(8,128)S(1)}, f32[40,128]{1,0:T(8,128)S(1)}, u32[]{:S(2)}, u32[]{:S(2)}) collective-permute-start(f32[40,128]{1,0:T(8,128)S(1)} %get-tuple-element.23), channel_id=1, source_target_pairs={{0,4},{4,0},{8,12},{12,8},{16,20},{20,16},{24,28},{28,24},{32,36},... | collective-permute-start | bytes 61448 | tf_op jit(solution)/shard_map/ppermute | solution.py:29
  72.1 2.6 %collective-permute-start.24 = (f32[40,128]{1,0:T(8,128)S(1)}, f32[40,128]{1,0:T(8,128)S(1)}, u32[]{:S(2)}, u32[]{:S(2)}) collective-permute-start(f32[40,128]{1,0:T(8,128)S(1)} %add.96), channel_id=1, source_target_pairs={{0,192},{4,196},{8,200},{12,204},{16,208},{20,212},{24,216},{28,22... | collective-permute-start | bytes 61448 | tf_op jit(solution)/shard_map/ppermute | solution.py:33
  73.0 3.8 %collective-permute-start.23 = (f32[40,128]{1,0:T(8,128)S(1)}, f32[40,128]{1,0:T(8,128)S(1)}, u32[]{:S(2)}, u32[]{:S(2)}) collective-permute-start(f32[40,128]{1,0:T(8,128)S(1)} %add.96), channel_id=1, source_target_pairs={{0,64},{4,68},{8,72},{12,76},{16,80},{20,84},{24,88},{28,92},{32,9... | collective-permute-start | bytes 61448 | tf_op jit(solution)/shard_map/ppermute | solution.py:33
  73.5 4.1 %collective-permute-start.22 = (f32[40,128]{1,0:T(8,128)S(1)}, f32[40,128]{1,0:T(8,128)S(1)}, u32[]{:S(2)}, u32[]{:S(2)}) collective-permute-start(f32[40,128]{1,0:T(8,128)S(1)} %add.96), channel_id=1, source_target_pairs={{0,128},{4,132},{8,136},{12,140},{16,144},{20,148},{24,152},{28,15... | collective-permute-start | bytes 61448 | tf_op jit(solution)/shard_map/ppermute | solution.py:33
  77.7 2.7 %collective-permute-start.25 = (f32[40,128]{1,0:T(8,128)S(1)}, f32[40,128]{1,0:T(8,128)S(1)}, u32[]{:S(2)}, u32[]{:S(2)}) collective-permute-start(f32[40,128]{1,0:T(8,128)S(1)} %add_add_fusion.1), channel_id=1, source_target_pairs={{0,8},{4,12},{8,0},{12,4},{16,24},{20,28},{24,16},{28,20},{32,40},... | collective-permute-start | bytes 61448 | tf_op jit(solution)/shard_map/ppermute | solution.py:41
  80.4 5.7 %collective-permute-start.28 = (f32[40,128]{1,0:T(8,128)S(1)}, f32[40,128]{1,0:T(8,128)S(1)}, u32[]{:S(2)}, u32[]{:S(2)}) collective-permute-start(f32[40,128]{1,0:T(8,128)S(1)} %add.100), channel_id=1, source_target_pairs={{0,48},{4,52},{8,56},{12,60},{16,0},{20,4},{24,8},{28,12},{32,16},... | collective-permute-start | bytes 61448 | tf_op jit(solution)/shard_map/ppermute | solution.py:37
  81.4 4.8 %collective-permute-start.27 = (f32[40,128]{1,0:T(8,128)S(1)}, f32[40,128]{1,0:T(8,128)S(1)}, u32[]{:S(2)}, u32[]{:S(2)}) collective-permute-start(f32[40,128]{1,0:T(8,128)S(1)} %add.100), channel_id=1, source_target_pairs={{0,16},{4,20},{8,24},{12,28},{16,32},{20,36},{24,40},{28,44},{32,4... | collective-permute-start | bytes 61448 | tf_op jit(solution)/shard_map/ppermute | solution.py:37
  82.9 6.5 %collective-permute-start.26 = (f32[40,128]{1,0:T(8,128)S(1)}, f32[40,128]{1,0:T(8,128)S(1)}, u32[]{:S(2)}, u32[]{:S(2)}) collective-permute-start(f32[40,128]{1,0:T(8,128)S(1)} %add.100), channel_id=1, source_target_pairs={{0,32},{4,36},{8,40},{12,44},{16,48},{20,52},{24,56},{28,60},{32,0... | collective-permute-start | bytes 61448 | tf_op jit(solution)/shard_map/ppermute | solution.py:37
  89.4 5.7 %collective-permute-start.29 = (f32[40,128]{1,0:T(8,128)S(1)}, f32[40,128]{1,0:T(8,128)S(1)}, u32[]{:S(2)}, u32[]{:S(2)}) collective-permute-start(f32[40,128]{1,0:T(8,128)S(1)} %add_add_fusion.mine), channel_id=1, source_target_pairs={{0,4},{4,0},{8,12},{12,8},{16,20},{20,16},{24,28},{28,24},{32,36},... | collective-permute-start | bytes 61448 | tf_op jit(solution)/shard_map/ppermute | solution.py:29

commit v3 on v2

--- a/solution.py
+++ b/solution.py
@@ -33,16 +33,16 @@
     return lax.ppermute(a, "coord", coord_pairs(lambda x, z, c: ((x + d) % NX, z, c)))
 
 
-def along_z(a, d):
-    return lax.ppermute(a, "coord", coord_pairs(lambda x, z, c: (x, (z + d) % NZ, c)))
-
-
-def z_partner(a):
-    return lax.ppermute(a, "coord", coord_pairs(lambda x, z, c: (x, z ^ 1, c)))
-
-
-def along_y(a, d):
-    return lax.ppermute(a, "dp", [(y, (y + d) % NY) for y in range(NY)])
+def swap_x(a, d):
+    return lax.ppermute(a, "coord", coord_pairs(lambda x, z, c: (x ^ d, z, c)))
+
+
+def swap_z(a, d):
+    return lax.ppermute(a, "coord", coord_pairs(lambda x, z, c: (x, z ^ d, c)))
+
+
+def swap_y(a, d):
+    return lax.ppermute(a, "dp", [(y, y ^ d) for y in range(NY)])
 
 
 def place_of_device():
@@ -106,11 +106,11 @@
         p = jnp.dot(a, p_buf[l, j], preferred_element_type=jnp.float32)
         b = bins[l, j]
         far_c = (b // HALF) ^ my_c
-        far_odd = (b ^ my_z) & 1
-        far_quad = ((b - (my_z ^ far_odd)) & (NZ - 1)) // 2
-        far_x = ((b // NZ) - my_x) & (NX - 1)
-        slot_a = ((far_x + 2) & (NX - 1)) * NZ + far_odd * (NZ // 2) + far_quad
-        slot_b = far_odd * (HALF // 2) + far_quad * NX + far_x
+        far_z = (b ^ my_z) & (NZ - 1)
+        far_z = ((far_z ^ ((far_z >> 2) & ~(far_z >> 1))) & 1) * (NZ // 2) + far_z // 2
+        b_x = b // NZ
+        slot_a = ((b_x - my_x + 2) & (NX - 1)) * NZ + far_z
+        slot_b = far_z * NX + ((b_x ^ my_x) & (NX - 1))
         out_a[far_c * HALF + slot_a] += p[:n_a]
         out_b[far_c * HALF + slot_b] += p[n_a:]
 
@@ -152,7 +152,7 @@
     layers, n_t, tok, r = h_t.shape
     n_v, cols = h_v.shape[1], g_t.shape[2]
     n = n_t + n_v
-    blk, slots, unroll = 16, 6, 20
+    blk, slots, unroll = 16, 6, 40
     in_hbm = pl.BlockSpec(memory_space=pltpu.HBM)
     return pl.pallas_call(
         functools.partial(feature_kernel, (layers, n_t, n_v, cols, blk, slots, unroll)),
@@ -191,8 +191,8 @@
     return total
 
 
-def along_z_pairs(a):
-    return add([a[0]] + [along_z(a[d], 2 * d) for d in (2, 1, 3)])
+def sum_quad(a):
+    return add([a[0]] + [swap_z(a[i], d) for i, d in ((2, 5), (1, 2), (3, 6))])
 
 
 def reduce_to_owner(f_a, f_b):
@@ -203,56 +203,49 @@
     half = f_a[:NZ] + first
     right, left = along_x(half[:mid], 1), along_x(half[mid:], -1)
     b = f_b[:HALF] + far_b
-    far_b = z_partner(b[HALF // 2 :])
+    far_b = swap_z(b[HALF // 2 :], 1)
     right, left, rest = lax.optimization_barrier((right, left, rest))
     half = f_a[NZ:HALF] + rest
     right = along_x(jnp.concatenate([half[2 * NZ : 2 * NZ + mid] + right, half[2 * NZ + mid :]]), 1)
     left = along_x(jnp.concatenate([half[:mid], half[mid:NZ] + left]), -1)
     b = (b[: HALF // 2] + far_b).reshape(mid, NX, *b.shape[1:])
-    b = along_z_pairs(b)
+    b = sum_quad(b)
     a = half[NZ : 2 * NZ] + right + left
-    a = a[:mid] + z_partner(a[mid:])
-    b = add([b[0]] + [along_x(b[d], d) for d in (2, 1, 3)])
-    return along_z_pairs(a), b
-
-
-def dots_kernel(n_v, rows_a, rows_b, v1, v2, v3, keep, send, val, dots, stats):
+    a = a[:mid] + swap_z(a[mid:], 1)
+    b = add([b[0]] + [swap_x(b[d], d) for d in (2, 1, 3)])
+    return sum_quad(a), b
+
+
+def dots_kernel(n_v, rows_a, rows_b, v1, v2, v3, out, val):
     y = lax.axis_index("dp")
-    _, _, c = place_of_device()
     n_b = rows_b.shape[0]
+    all_v = NY * n_v
     train = rows_a[...]
     if n_b > n_v:
         train = jnp.concatenate([train, rows_b[0 : n_b - n_v, :]])
     val[pl.ds(pl.multiple_of(y * n_v, n_v), n_v), :] = rows_b[n_b - n_v : n_b, :]
     for d, part in ((1, v1), (2, v2), (3, v3)):
-        val[pl.ds(pl.multiple_of(((y - d) & (NY - 1)) * n_v, n_v), n_v), :] = part[...]
+        val[pl.ds(pl.multiple_of((y ^ d) * n_v, n_v), n_v), :] = part[...]
     v = val[...]
     contract = lambda a, b: lax.dot_general(
         a, b, (((1,), (1,)), ((), ())), precision=lax.Precision.HIGHEST, preferred_element_type=jnp.float32
     )
-    dots[...] = contract(v, train)
+    out[0:all_v, :] = contract(v, train)
     ones = jnp.ones((8, BW), jnp.float32)
-    stats[0] = contract(ones, train * train)
-    stats[1] = jnp.zeros_like(stats[1])
-    stats[1, :, 0 : NY * n_v] = contract(ones, v * v)
-    rows = NY * n_v // NC
-    for ref, h in ((keep, c), (send, 1 - c)):
-        ref[0:rows, :] = dots[pl.ds(pl.multiple_of(h * rows, rows), rows), :]
-        ref[rows : rows + 8, :] = stats[h]
-
-
-def scores_kernel(mine, other, tasks, cos_out, score_out, dots, stats):
-    _, _, c = place_of_device()
+    out[all_v : all_v + 8, :] = contract(ones, train * train)
+    out[all_v + 8 : all_v + 16, :] = jnp.zeros((8, out.shape[1]), jnp.float32)
+    out[all_v + 8 : all_v + 16, 0:all_v] = contract(ones, v * v)
+
+
+def scores_kernel(*refs):
+    *parts, tasks, cos_out, score_out = refs
     n_v = tasks.shape[1]
-    rows = n_v // NC
-    for ref, h in ((mine, c), (other, 1 - c)):
-        dots[pl.ds(pl.multiple_of(h * rows, rows), rows), :] = ref[0:rows, :]
-        stats[h] = ref[rows : rows + 8, :]
+    total = add([part[...] for part in parts])
     on_diagonal = lax.broadcasted_iota(jnp.int32, (n_v, n_v), 0) == lax.broadcasted_iota(jnp.int32, (n_v, n_v), 1)
-    train_norm = jnp.sqrt(stats[0, 0:1, :] + 1e-06)
-    val_norm_row = jnp.sqrt(stats[1, 0:1, 0:n_v] + 1e-06)
+    train_norm = jnp.sqrt(total[n_v : n_v + 1, :] + 1e-06)
+    val_norm_row = jnp.sqrt(total[n_v + 8 : n_v + 9, 0:n_v] + 1e-06)
     val_norm = jnp.sum(jnp.where(on_diagonal, val_norm_row, 0.0), axis=1, keepdims=True)
-    cos = dots[...] / (train_norm * val_norm)
+    cos = total[0:n_v, :] / (train_norm * val_norm)
     cos_out[...] = cos
     task_row = tasks[...].astype(jnp.float32)
     task = jnp.sum(jnp.where(on_diagonal, task_row, 0.0), axis=1, keepdims=True)
@@ -271,35 +264,25 @@
     )
     rows_a, rows_b = reduce_to_owner(f_a, f_b)
     v = rows_b[ROWS_B:]
-    others = [along_y(v, d) for d in (1, 2, 3)]
-    part = pltpu.VMEM((all_v // NC + 8, n_t), jnp.float32)
-    keep, send = pl.pallas_call(
+    others = [swap_y(v, d) for d in (1, 2, 3)]
+    a = pl.pallas_call(
         functools.partial(dots_kernel, n_v),
-        out_shape=(part, part),
-        scratch_shapes=[
-            pltpu.VMEM((all_v, BW), jnp.float32),
-            pltpu.VMEM((all_v, n_t), jnp.float32),
-            pltpu.VMEM((NC, 8, n_t), jnp.float32),
-        ],
+        out_shape=pltpu.VMEM((all_v + 16, n_t), jnp.float32),
+        scratch_shapes=[pltpu.VMEM((all_v, BW), jnp.float32)],
         name="dots",
     )(*map(in_vmem, (rows_a, rows_b, *others)))
-    a = keep + to_core(send)
-    got = [along_x(a, d) for d in (2, 1, 3)]
-    a = a + got[0] + got[1] + got[2]
-    a = a + z_partner(a)
-    a = add([a] + [along_z(a, d) for d in (4, 2, 6)])
+    a = add([a] + [swap_x(a, d) for d in (2, 1, 3)])
+    a = add([a] + [swap_z(a, d) for d in (3, 2, 1)])
+    a = a + swap_z(a, 6)
+    parts = (a, to_core(a))
     cos_t, scores_t = pl.pallas_call(
         scores_kernel,
         out_shape=(
             jax.ShapeDtypeStruct((all_v, n_t), jnp.float32),
             jax.ShapeDtypeStruct((NTASK, n_t), jnp.float32),
         ),
-        scratch_shapes=[
-            pltpu.VMEM((all_v, n_t), jnp.float32),
-            pltpu.VMEM((NC, 8, n_t), jnp.float32),
-        ],
         name="scores",
-    )(in_vmem(a), in_vmem(to_core(a)), tasks.reshape(1, all_v))
+    )(*map(in_vmem, parts), tasks.reshape(1, all_v))
     return cos_t.T, scores_t.T
 
 

time: 96.6 us -> 92.9 us (0.962)
  starting transfers between devices: 53.3 us -> 47.8 us
  waiting for transfers between devices: 23.6 us -> 25.7 us
    ppermute x10 -> x4, starting transfers between devices: 10.2 us -> 3.16 us  [along_x(): lax.ppermute(a, 'coord', coord_pairs(lambda x, z, c: ((x + d) % NX, z, c)))]
    ppermute x15 -> x21, waiting for transfers between devices: 9.26 us -> 14 us  [the longest x12 9.7 us: swap_z(): return lax.ppermute(a, 'coord', coord_pairs(lambda x, z, c: (x, z ^ d, c)))]
    ppermute x15 -> x21, starting transfers between devices: 28.5 us -> 31 us  [the longest x12 20.9 us: swap_z(): return lax.ppermute(a, 'coord', coord_pairs(lambda x, z, c: (x, z ^ d, c)))]
    ppermute x10 -> x4, waiting for transfers between devices: 9.61 us -> 7.82 us  [along_x(): lax.ppermute(a, 'coord', coord_pairs(lambda x, z, c: ((x + d) % NX, z, c)))]
    ppermute x5 -> x4, starting transfers between devices: 14.5 us -> 13.6 us  [to_core(): return lax.ppermute(a, 'coord', coord_pairs(lambda x, z, c: (x, z, 1 - c)))]
    ppermute x5 -> x4, waiting for transfers between devices: 4.73 us -> 3.91 us  [to_core(): return lax.ppermute(a, 'coord', coord_pairs(lambda x, z, c: (x, z, 1 - c)))]
  transfers between devices with their start and end apart: 30 -> 29, of which waited for: 18 -> 17; matrix products, arithmetic and copies ran while one was open for 1% -> 1% of each run, Pallas kernels for 0% -> 0%
where the time goes in v3:
time: 92.9 us; the launch traced here: 92.8 us
  starting transfers between devices  47.8 us (51%)
  waiting for transfers between devices  25.7 us (28%)
  Pallas kernels  17.4 us (19%)
    ppermute x12, starting transfers between devices, swap_z(): return lax.ppermute(a, 'coord', coord_pairs(lambda x, z, c: (x, z ^ d, c)))  20.9 us
    pallas_call x1, Pallas kernels, local_features(): pl.pallas_call(functools.partial(feature_kernel, (layers, n_t, n_v, cols,...  15.7 us
    ppermute x4, starting transfers between devices, to_core(): return lax.ppermute(a, 'coord', coord_pairs(lambda x, z, c: (x, z, 1 - c)))  13.6 us
    ppermute x12, waiting for transfers between devices, swap_z(): return lax.ppermute(a, 'coord', coord_pairs(lambda x, z, c: (x, z ^ d, c)))  9.7 us
    ppermute x4, waiting for transfers between devices, along_x(): lax.ppermute(a, 'coord', coord_pairs(lambda x, z, c: ((x + d) % NX, z, c)))  7.82 us
    ppermute x6, starting transfers between devices, swap_x(): return lax.ppermute(a, 'coord', coord_pairs(lambda x, z, c: (x ^ d, z, c)))  6.64 us
    ppermute x4, waiting for transfers between devices, to_core(): return lax.ppermute(a, 'coord', coord_pairs(lambda x, z, c: (x, z, 1 - c)))  3.91 us
    ppermute x3, starting transfers between devices, swap_y(): return lax.ppermute(a, 'dp', [(y, y ^ d) for y in range(NY)])  3.5 us
  transfers between devices with their start and end apart: 29, of which 17 were waited for; matrix products, arithmetic and copies ran while one was open for 1% of the time, Pallas kernels for 0%

profile of v3, /device:TPU:1, one launch (start us, length us, event | category | flops | bytes accessed | tf_op | source)
XLA Modules:
  0.0 92.8 jit_solution(6359901742436923662)
XLA Ops:
  0.6 15.7 %features.1 = (f32[64,112,128]{2,1,0:T(8,128)S(1)}, f32[64,32,128]{2,1,0:T(8,128)S(1)}) custom-call(s32[2,80]{1,0:T(2,128)} %bins_hbm.1, bf16[2,128,256,128]{3,2,1,0:T(8,128)(2,1)} %h_t.1, bf16[2,128,80,256]{3,2,1,0:T(8,128)(2,1)} %bitcast.33, bf16[2,16,256,128]{3,2,1,0:T(8,128)(2,1)} %h_v.1, bf16[2,16,80,256]{3,2,1,0:T(8,128)(2,1)} %bitcast.34, ...), custom_call_target="tpu_custom_call" | custom-call | tf_op jit(solution)/shard_map/features/pallas_call | solution.py:157
  16.4 3.3 %collective-permute-start = (f32[8,112,128]{2,1,0:T(8,128)S(1)}, f32[8,112,128]{2,1,0:T(8,128)S(1)}, u32[]{:S(2)}, u32[]{:S(2)}) collective-permute-start(f32[8,112,128]{2,1,0:T(8,128)S(1)} %slice.96), channel_id=1, source_target_pairs={{0,4},{4,0},{8,12},{12,8},{16,20},{20,16},{24,28},{28,24},{32,36},... | collective-permute-start | bytes 1376264 | tf_op jit(solution)/shard_map/ppermute | solution.py:29
  19.7 0.1 slice.97
  19.8 1.3 %collective-permute-done = f32[8,112,128]{2,1,0:T(8,128)S(1)} collective-permute-done((f32[8,112,128]{2,1,0:T(8,128)S(1)}, f32[8,112,128]{2,1,0:T(8,128)S(1)}, u32[]{:S(2)}, u32[]{:S(2)}) %collective-permute-start) | collective-permute-done | bytes 458784 | tf_op jit(solution)/shard_map/ppermute | solution.py:29
  21.1 0.4 collective-permute-start.3
  21.5 0.1 collective-permute-start.10
  21.8 0.8 collective-permute-start.2
  22.6 0.7 collective-permute-start.1
  23.3 1.7 %collective-permute-done.10 = f32[32,32,128]{2,1,0:T(8,128)S(1)} collective-permute-done((f32[32,32,128]{2,1,0:T(8,128)S(1)}, f32[32,32,128]{2,1,0:T(8,128)S(1)}, u32[]{:S(2)}, u32[]{:S(2)}) %collective-permute-start.10) | collective-permute-done | bytes 524320 | tf_op jit(solution)/shard_map/ppermute | solution.py:29
  25.0 0.1 slice_add_fusion.1
  25.1 0.1 collective-permute-start.11
  25.2 3.4 %collective-permute-done.2 = f32[4,112,128]{2,1,0:T(8,128)S(1)} collective-permute-done((f32[4,112,128]{2,1,0:T(8,128)S(1)}, f32[4,112,128]{2,1,0:T(8,128)S(1)}, u32[]{:S(2)}, u32[]{:S(2)}) %collective-permute-start.2) | collective-permute-done | bytes 229408 | tf_op jit(solution)/shard_map/ppermute | solution.py:33
  28.6 1.6 %collective-permute-done.1 = f32[4,112,128]{2,1,0:T(8,128)S(1)} collective-permute-done((f32[4,112,128]{2,1,0:T(8,128)S(1)}, f32[4,112,128]{2,1,0:T(8,128)S(1)}, u32[]{:S(2)}, u32[]{:S(2)}) %collective-permute-start.1) | collective-permute-done | bytes 229408 | tf_op jit(solution)/shard_map/ppermute | solution.py:33
  30.3 0.0 collective-permute-done.3
  30.3 0.2 slice_add_fusion
  30.5 0.1 slice_add_fusion.7
  30.6 0.4 collective-permute-start.5
  31.0 1.2 %collective-permute-start.4 = (f32[8,112,128]{2,1,0:T(8,128)S(1)}, f32[8,112,128]{2,1,0:T(8,128)S(1)}, u32[]{:S(2)}, u32[]{:S(2)}) collective-permute-start(f32[8,112,128]{2,1,0:T(8,128)S(1)} %pad_maximum_fusion), channel_id=1, source_target_pairs={{0,64},{4,68},{8,72},{12,76},{16,80},{20,84},{24,88},{28,92},{32,9... | collective-permute-start | bytes 1376264 | tf_op jit(solution)/shard_map/ppermute | solution.py:33
  32.3 0.5 collective-permute-done.11
  32.8 6.1 %collective-permute-start.12 = (f32[4,32,128]{2,1,0:T(8,128)S(1)}, f32[4,32,128]{2,1,0:T(8,128)S(1)}, u32[]{:S(2)}, u32[]{:S(2)}) collective-permute-start(f32[4,32,128]{2,1,0:T(8,128)S(1)} %get-tuple-element.28), channel_id=1, source_target_pairs={{0,40},{4,44},{8,32},{12,36},{16,56},{20,60},{24,48},{28,52},{32,8... | collective-permute-start | bytes 196616 | tf_op jit(solution)/shard_map/ppermute | solution.py:41
  38.9 0.3 collective-permute-start.14
  39.1 0.9 collective-permute-start.13
  40.1 1.1 %collective-permute-done.5 = f32[8,112,128]{2,1,0:T(8,128)S(1)} collective-permute-done((f32[8,112,128]{2,1,0:T(8,128)S(1)}, f32[8,112,128]{2,1,0:T(8,128)S(1)}, u32[]{:S(2)}, u32[]{:S(2)}) %collective-permute-start.5) | collective-permute-done | bytes 458784 | tf_op jit(solution)/shard_map/ppermute | solution.py:33
  41.2 1.7 %collective-permute-done.4 = f32[8,112,128]{2,1,0:T(8,128)S(1)} collective-permute-done((f32[8,112,128]{2,1,0:T(8,128)S(1)}, f32[8,112,128]{2,1,0:T(8,128)S(1)}, u32[]{:S(2)}, u32[]{:S(2)}) %collective-permute-start.4) | collective-permute-done | bytes 458784 | tf_op jit(solution)/shard_map/ppermute | solution.py:33
  42.8 0.1 fusion
  43.0 1.7 %collective-permute-start.6 = (f32[4,112,128]{2,1,0:T(8,128)S(1)}, f32[4,112,128]{2,1,0:T(8,128)S(1)}, u32[]{:S(2)}, u32[]{:S(2)}) collective-permute-start(f32[4,112,128]{2,1,0:T(8,128)S(1)} %slice.132), channel_id=1, source_target_pairs={{0,8},{4,12},{8,0},{12,4},{16,24},{20,28},{24,16},{28,20},{32,40},... | collective-permute-start | bytes 688136 | tf_op jit(solution)/shard_map/ppermute | solution.py:41
  44.7 0.0 collective-permute-done.12
  44.7 0.0 collective-permute-done.14
  44.7 0.3 collective-permute-done.13
  45.1 1.3 %collective-permute-start.15 = (f32[32,128]{1,0:T(8,128)S(1)}, f32[32,128]{1,0:T(8,128)S(1)}, u32[]{:S(2)}, u32[]{:S(2)}) collective-permute-start(f32[32,128]{1,0:T(8,128)S(1)} %get-tuple-element.34), channel_id=1, source_target_pairs={{0,128},{4,132},{8,136},{12,140},{16,144},{20,148},{24,152},{28,15... | collective-permute-start | bytes 49160 | tf_op jit(solution)/shard_map/ppermute | solution.py:37
  46.4 1.2 %collective-permute-start.17 = (f32[32,128]{1,0:T(8,128)S(1)}, f32[32,128]{1,0:T(8,128)S(1)}, u32[]{:S(2)}, u32[]{:S(2)}) collective-permute-start(f32[32,128]{1,0:T(8,128)S(1)} %get-tuple-element.35), channel_id=1, source_target_pairs={{0,192},{4,196},{8,200},{12,204},{16,208},{20,212},{24,216},{28,22... | collective-permute-start | bytes 49160 | tf_op jit(solution)/shard_map/ppermute | solution.py:37
  47.5 0.3 collective-permute-start.16
  47.8 1.7 %collective-permute-done.6 = f32[4,112,128]{2,1,0:T(8,128)S(1)} collective-permute-done((f32[4,112,128]{2,1,0:T(8,128)S(1)}, f32[4,112,128]{2,1,0:T(8,128)S(1)}, u32[]{:S(2)}, u32[]{:S(2)}) %collective-permute-start.6) | collective-permute-done | bytes 229408 | tf_op jit(solution)/shard_map/ppermute | solution.py:41
  49.6 5.0 %collective-permute-start.7 = (f32[112,128]{1,0:T(8,128)S(1)}, f32[112,128]{1,0:T(8,128)S(1)}, u32[]{:S(2)}, u32[]{:S(2)}) collective-permute-start(f32[112,128]{1,0:T(8,128)S(1)} %get-tuple-element.31), channel_id=1, source_target_pairs={{0,40},{4,44},{8,32},{12,36},{16,56},{20,60},{24,48},{28,52},{32,8... | collective-permute-start | bytes 172040 | tf_op jit(solution)/shard_map/ppermute | solution.py:41
  54.5 0.3 collective-permute-start.9
  54.8 0.0 collective-permute-done.15
  54.8 0.9 collective-permute-start.8
  55.7 0.0 collective-permute-done.17
  55.7 0.0 collective-permute-done.16
  55.8 2.8 %collective-permute-start.20 = (f32[16,128]{1,0:T(8,128)S(1)}, f32[16,128]{1,0:T(8,128)S(1)}, u32[]{:S(2)}, u32[]{:S(2)}) collective-permute-start(f32[16,128]{1,0:T(8,128)S(1)} %slice.147), channel_id=1, source_target_pairs={{0,3},{1,2},{2,1},{3,0},{4,7},{5,6},{6,5},{7,4},{8,11},{9,10},{10,... | collective-permute-start | bytes 24584 | tf_op jit(solution)/shard_map/ppermute | solution.py:45
  58.6 0.3 collective-permute-start.19
  58.9 0.0 collective-permute-done.7
  58.9 0.3 collective-permute-start.18
  59.3 0.8 collective-permute-done.9
  60.1 0.0 collective-permute-done.8
  60.1 0.0 collective-permute-done.20.v3
  60.1 2.5 %collective-permute-done.19.v2 = f32[16,128]{1,0:T(8,128)S(1)} collective-permute-done((f32[16,128]{1,0:T(8,128)S(1)}, f32[16,128]{1,0:T(8,128)S(1)}, u32[]{:S(2)}, u32[]{:S(2)}) %collective-permute-start.19) | collective-permute-done | bytes 8224 | tf_op jit(solution)/shard_map/ppermute | solution.py:45
  62.6 0.0 collective-permute-done.18.v1
  62.6 0.4 dots.1
  62.9 0.3 collective-permute-start.23
  63.3 0.0 collective-permute-start.22
  63.3 3.6 %collective-permute-start.21 = (f32[80,128]{1,0:T(8,128)S(1)}, f32[80,128]{1,0:T(8,128)S(1)}, u32[]{:S(2)}, u32[]{:S(2)}) collective-permute-start(f32[80,128]{1,0:T(8,128)S(1)} %dots.1), channel_id=1, source_target_pairs={{0,128},{4,132},{8,136},{12,140},{16,144},{20,148},{24,152},{28,15... | collective-permute-start | bytes 122888 | tf_op jit(solution)/shard_map/ppermute | solution.py:37
  66.9 0.2 collective-permute-done.23
  67.1 1.6 %collective-permute-done.21 = f32[80,128]{1,0:T(8,128)S(1)} collective-permute-done((f32[80,128]{1,0:T(8,128)S(1)}, f32[80,128]{1,0:T(8,128)S(1)}, u32[]{:S(2)}, u32[]{:S(2)}) %collective-permute-start.21) | collective-permute-done | bytes 40992 | tf_op jit(solution)/shard_map/ppermute | solution.py:37
  68.7 1.3 %collective-permute-start.26 = (f32[80,128]{1,0:T(8,128)S(1)}, f32[80,128]{1,0:T(8,128)S(1)}, u32[]{:S(2)}, u32[]{:S(2)}) collective-permute-start(f32[80,128]{1,0:T(8,128)S(1)} %add_add_fusion.1), channel_id=1, source_target_pairs={{0,8},{4,12},{8,0},{12,4},{16,24},{20,28},{24,16},{28,20},{32,40},... | collective-permute-start | bytes 122888 | tf_op jit(solution)/shard_map/ppermute | solution.py:41
  70.0 0.7 collective-permute-start.25
  70.7 1.6 %collective-permute-start.24 = (f32[80,128]{1,0:T(8,128)S(1)}, f32[80,128]{1,0:T(8,128)S(1)}, u32[]{:S(2)}, u32[]{:S(2)}) collective-permute-start(f32[80,128]{1,0:T(8,128)S(1)} %add_add_fusion.1), channel_id=1, source_target_pairs={{0,24},{4,28},{8,16},{12,20},{16,8},{20,12},{24,0},{28,4},{32,56},... | collective-permute-start | bytes 122888 | tf_op jit(solution)/shard_map/ppermute | solution.py:41
  72.3 1.8 %collective-permute-done.25 = f32[80,128]{1,0:T(8,128)S(1)} collective-permute-done((f32[80,128]{1,0:T(8,128)S(1)}, f32[80,128]{1,0:T(8,128)S(1)}, u32[]{:S(2)}, u32[]{:S(2)}) %collective-permute-start.25) | collective-permute-done | bytes 40992 | tf_op jit(solution)/shard_map/ppermute | solution.py:41
  74.2 1.5 %collective-permute-done.24 = f32[80,128]{1,0:T(8,128)S(1)} collective-permute-done((f32[80,128]{1,0:T(8,128)S(1)}, f32[80,128]{1,0:T(8,128)S(1)}, u32[]{:S(2)}, u32[]{:S(2)}) %collective-permute-start.24) | collective-permute-done | bytes 40992 | tf_op jit(solution)/shard_map/ppermute | solution.py:41
  75.6 2.0 %collective-permute-start.27 = (f32[80,128]{1,0:T(8,128)S(1)}, f32[80,128]{1,0:T(8,128)S(1)}, u32[]{:S(2)}, u32[]{:S(2)}) collective-permute-start(f32[80,128]{1,0:T(8,128)S(1)} %add_add_fusion), channel_id=1, source_target_pairs={{0,48},{4,52},{8,56},{12,60},{16,32},{20,36},{24,40},{28,44},{32,1... | collective-permute-start | bytes 122888 | tf_op jit(solution)/shard_map/ppermute | solution.py:41
  77.7 3.0 %collective-permute-done.27 = f32[80,128]{1,0:T(8,128)S(1)} collective-permute-done((f32[80,128]{1,0:T(8,128)S(1)}, f32[80,128]{1,0:T(8,128)S(1)}, u32[]{:S(2)}, u32[]{:S(2)}) %collective-permute-start.27) | collective-permute-done | bytes 40992 | tf_op jit(solution)/shard_map/ppermute | solution.py:41
  80.7 9.8 %collective-permute-start.28 = (f32[80,128]{1,0:T(8,128)S(1)}, f32[80,128]{1,0:T(8,128)S(1)}, u32[]{:S(2)}, u32[]{:S(2)}) collective-permute-start(f32[80,128]{1,0:T(8,128)S(1)} %add.99.refs_0_), channel_id=1, source_target_pairs={{0,4},{4,0},{8,12},{12,8},{16,20},{20,16},{24,28},{28,24},{32,36},... | collective-permute-start | bytes 122888 | tf_op jit(solution)/shard_map/ppermute | solution.py:29
  90.5 0.9 collective-permute-done.28.refs_1_
  91.4 1.4 %scores.1 = (f32[64,128]{1,0:T(8,128)}, f32[3,128]{1,0:T(4,128)}) custom-call(f32[80,128]{1,0:T(8,128)S(1)} %add.99.refs_0_, f32[80,128]{1,0:T(8,128)S(1)} %collective-permute-done.28.refs_1_, s32[1,64]{1,0:T(1,128)} %bitcast.35), custom_call_target="tpu_custom_call" | custom-call | tf_op jit(solution)/shard_map/scores/pallas_call | solution.py:278
  (22 shorter events, 0.4 us)
Async XLA Ops:
  16.4 4.8 %collective-permute-start = (f32[8,112,128]{2,1,0:T(8,128)S(1)}, f32[8,112,128]{2,1,0:T(8,128)S(1)}, u32[]{:S(2)}, u32[]{:S(2)}) collective-permute-start(f32[8,112,128]{2,1,0:T(8,128)S(1)} %slice.96), channel_id=1, source_target_pairs={{0,4},{4,0},{8,12},{12,8},{16,20},{20,16},{24,28},{28,24},{32,36},... | collective-permute-start | bytes 1376264 | tf_op jit(solution)/shard_map/ppermute | solution.py:29
  21.1 9.1 %collective-permute-start.3 = (f32[24,112,128]{2,1,0:T(8,128)S(1)}, f32[24,112,128]{2,1,0:T(8,128)S(1)}, u32[]{:S(2)}, u32[]{:S(2)}) collective-permute-start(f32[24,112,128]{2,1,0:T(8,128)S(1)} %slice.97), channel_id=1, source_target_pairs={{0,4},{4,0},{8,12},{12,8},{16,20},{20,16},{24,28},{28,24},{32,36},... | collective-permute-start | bytes 4128776 | tf_op jit(solution)/shard_map/ppermute | solution.py:29
  21.5 3.5 %collective-permute-start.10 = (f32[32,32,128]{2,1,0:T(8,128)S(1)}, f32[32,32,128]{2,1,0:T(8,128)S(1)}, u32[]{:S(2)}, u32[]{:S(2)}) collective-permute-start(f32[32,32,128]{2,1,0:T(8,128)S(1)} %slice.98), channel_id=1, source_target_pairs={{0,4},{4,0},{8,12},{12,8},{16,20},{20,16},{24,28},{28,24},{32,36},... | collective-permute-start | bytes 1572872 | tf_op jit(solution)/shard_map/ppermute | solution.py:29
  21.8 6.9 %collective-permute-start.2 = (f32[4,112,128]{2,1,0:T(8,128)S(1)}, f32[4,112,128]{2,1,0:T(8,128)S(1)}, u32[]{:S(2)}, u32[]{:S(2)}) collective-permute-start(f32[4,112,128]{2,1,0:T(8,128)S(1)} %get-tuple-element.26), channel_id=1, source_target_pairs={{0,192},{4,196},{8,200},{12,204},{16,208},{20,212},{24,216},{28,22... | collective-permute-start | bytes 688136 | tf_op jit(solution)/shard_map/ppermute | solution.py:33
  22.6 7.7 %collective-permute-start.1 = (f32[4,112,128]{2,1,0:T(8,128)S(1)}, f32[4,112,128]{2,1,0:T(8,128)S(1)}, u32[]{:S(2)}, u32[]{:S(2)}) collective-permute-start(f32[4,112,128]{2,1,0:T(8,128)S(1)} %get-tuple-element.27), channel_id=1, source_target_pairs={{0,64},{4,68},{8,72},{12,76},{16,80},{20,84},{24,88},{28,92},{32,9... | collective-permute-start | bytes 688136 | tf_op jit(solution)/shard_map/ppermute | solution.py:33
  25.1 7.6 %collective-permute-start.11 = (f32[16,32,128]{2,1,0:T(8,128)S(1)}, f32[16,32,128]{2,1,0:T(8,128)S(1)}, u32[]{:S(2)}, u32[]{:S(2)}) collective-permute-start(f32[16,32,128]{2,1,0:T(8,128)S(1)} %slice.138), channel_id=1, source_target_pairs={{0,8},{4,12},{8,0},{12,4},{16,24},{20,28},{24,16},{28,20},{32,40},... | collective-permute-start | bytes 786440 | tf_op jit(solution)/shard_map/ppermute | solution.py:41
  30.6 10.6 %collective-permute-start.5 = (f32[8,112,128]{2,1,0:T(8,128)S(1)}, f32[8,112,128]{2,1,0:T(8,128)S(1)}, u32[]{:S(2)}, u32[]{:S(2)}) collective-permute-start(f32[8,112,128]{2,1,0:T(8,128)S(1)} %pad_maximum_fusion.1), channel_id=1, source_target_pairs={{0,192},{4,196},{8,200},{12,204},{16,208},{20,212},{24,216},{28,22... | collective-permute-start | bytes 1376264 | tf_op jit(solution)/shard_map/ppermute | solution.py:33
  31.0 11.8 %collective-permute-start.4 = (f32[8,112,128]{2,1,0:T(8,128)S(1)}, f32[8,112,128]{2,1,0:T(8,128)S(1)}, u32[]{:S(2)}, u32[]{:S(2)}) collective-permute-start(f32[8,112,128]{2,1,0:T(8,128)S(1)} %pad_maximum_fusion), channel_id=1, source_target_pairs={{0,64},{4,68},{8,72},{12,76},{16,80},{20,84},{24,88},{28,92},{32,9... | collective-permute-start | bytes 1376264 | tf_op jit(solution)/shard_map/ppermute | solution.py:33
  32.8 11.9 %collective-permute-start.12 = (f32[4,32,128]{2,1,0:T(8,128)S(1)}, f32[4,32,128]{2,1,0:T(8,128)S(1)}, u32[]{:S(2)}, u32[]{:S(2)}) collective-permute-start(f32[4,32,128]{2,1,0:T(8,128)S(1)} %get-tuple-element.28), channel_id=1, source_target_pairs={{0,40},{4,44},{8,32},{12,36},{16,56},{20,60},{24,48},{28,52},{32,8... | collective-permute-start | bytes 196616 | tf_op jit(solution)/shard_map/ppermute | solution.py:41
  38.9 5.8 %collective-permute-start.14 = (f32[4,32,128]{2,1,0:T(8,128)S(1)}, f32[4,32,128]{2,1,0:T(8,128)S(1)}, u32[]{:S(2)}, u32[]{:S(2)}) collective-permute-start(f32[4,32,128]{2,1,0:T(8,128)S(1)} %get-tuple-element.29), channel_id=1, source_target_pairs={{0,48},{4,52},{8,56},{12,60},{16,32},{20,36},{24,40},{28,44},{32,1... | collective-permute-start | bytes 196616 | tf_op jit(solution)/shard_map/ppermute | solution.py:41
  39.1 5.9 %collective-permute-start.13 = (f32[4,32,128]{2,1,0:T(8,128)S(1)}, f32[4,32,128]{2,1,0:T(8,128)S(1)}, u32[]{:S(2)}, u32[]{:S(2)}) collective-permute-start(f32[4,32,128]{2,1,0:T(8,128)S(1)} %get-tuple-element.30), channel_id=1, source_target_pairs={{0,16},{4,20},{8,24},{12,28},{16,0},{20,4},{24,8},{28,12},{32,48},... | collective-permute-start | bytes 196616 | tf_op jit(solution)/shard_map/ppermute | solution.py:41
  43.0 6.5 %collective-permute-start.6 = (f32[4,112,128]{2,1,0:T(8,128)S(1)}, f32[4,112,128]{2,1,0:T(8,128)S(1)}, u32[]{:S(2)}, u32[]{:S(2)}) collective-permute-start(f32[4,112,128]{2,1,0:T(8,128)S(1)} %slice.132), channel_id=1, source_target_pairs={{0,8},{4,12},{8,0},{12,4},{16,24},{20,28},{24,16},{28,20},{32,40},... | collective-permute-start | bytes 688136 | tf_op jit(solution)/shard_map/ppermute | solution.py:41
  45.1 9.8 %collective-permute-start.15 = (f32[32,128]{1,0:T(8,128)S(1)}, f32[32,128]{1,0:T(8,128)S(1)}, u32[]{:S(2)}, u32[]{:S(2)}) collective-permute-start(f32[32,128]{1,0:T(8,128)S(1)} %get-tuple-element.34), channel_id=1, source_target_pairs={{0,128},{4,132},{8,136},{12,140},{16,144},{20,148},{24,152},{28,15... | collective-permute-start | bytes 49160 | tf_op jit(solution)/shard_map/ppermute | solution.py:37
  46.4 9.4 %collective-permute-start.17 = (f32[32,128]{1,0:T(8,128)S(1)}, f32[32,128]{1,0:T(8,128)S(1)}, u32[]{:S(2)}, u32[]{:S(2)}) collective-permute-start(f32[32,128]{1,0:T(8,128)S(1)} %get-tuple-element.35), channel_id=1, source_target_pairs={{0,192},{4,196},{8,200},{12,204},{16,208},{20,212},{24,216},{28,22... | collective-permute-start | bytes 49160 | tf_op jit(solution)/shard_map/ppermute | solution.py:37
  47.5 8.2 %collective-permute-start.16 = (f32[32,128]{1,0:T(8,128)S(1)}, f32[32,128]{1,0:T(8,128)S(1)}, u32[]{:S(2)}, u32[]{:S(2)}) collective-permute-start(f32[32,128]{1,0:T(8,128)S(1)} %get-tuple-element.36), channel_id=1, source_target_pairs={{0,64},{4,68},{8,72},{12,76},{16,80},{20,84},{24,88},{28,92},{32,9... | collective-permute-start | bytes 49160 | tf_op jit(solution)/shard_map/ppermute | solution.py:37
  49.6 9.4 %collective-permute-start.7 = (f32[112,128]{1,0:T(8,128)S(1)}, f32[112,128]{1,0:T(8,128)S(1)}, u32[]{:S(2)}, u32[]{:S(2)}) collective-permute-start(f32[112,128]{1,0:T(8,128)S(1)} %get-tuple-element.31), channel_id=1, source_target_pairs={{0,40},{4,44},{8,32},{12,36},{16,56},{20,60},{24,48},{28,52},{32,8... | collective-permute-start | bytes 172040 | tf_op jit(solution)/shard_map/ppermute | solution.py:41
  54.5 5.5 %collective-permute-start.9 = (f32[112,128]{1,0:T(8,128)S(1)}, f32[112,128]{1,0:T(8,128)S(1)}, u32[]{:S(2)}, u32[]{:S(2)}) collective-permute-start(f32[112,128]{1,0:T(8,128)S(1)} %get-tuple-element.32), channel_id=1, source_target_pairs={{0,48},{4,52},{8,56},{12,60},{16,32},{20,36},{24,40},{28,44},{32,1... | collective-permute-start | bytes 172040 | tf_op jit(solution)/shard_map/ppermute | solution.py:41
  54.8 5.3 %collective-permute-start.8 = (f32[112,128]{1,0:T(8,128)S(1)}, f32[112,128]{1,0:T(8,128)S(1)}, u32[]{:S(2)}, u32[]{:S(2)}) collective-permute-start(f32[112,128]{1,0:T(8,128)S(1)} %get-tuple-element.33), channel_id=1, source_target_pairs={{0,16},{4,20},{8,24},{12,28},{16,0},{20,4},{24,8},{28,12},{32,48},... | collective-permute-start | bytes 172040 | tf_op jit(solution)/shard_map/ppermute | solution.py:41
  55.8 4.3 %collective-permute-start.20 = (f32[16,128]{1,0:T(8,128)S(1)}, f32[16,128]{1,0:T(8,128)S(1)}, u32[]{:S(2)}, u32[]{:S(2)}) collective-permute-start(f32[16,128]{1,0:T(8,128)S(1)} %slice.147), channel_id=1, source_target_pairs={{0,3},{1,2},{2,1},{3,0},{4,7},{5,6},{6,5},{7,4},{8,11},{9,10},{10,... | collective-permute-start | bytes 24584 | tf_op jit(solution)/shard_map/ppermute | solution.py:45
  58.6 4.0 %collective-permute-start.19 = (f32[16,128]{1,0:T(8,128)S(1)}, f32[16,128]{1,0:T(8,128)S(1)}, u32[]{:S(2)}, u32[]{:S(2)}) collective-permute-start(f32[16,128]{1,0:T(8,128)S(1)} %slice.147), channel_id=1, source_target_pairs={{0,2},{1,3},{2,0},{3,1},{4,6},{5,7},{6,4},{7,5},{8,10},{9,11},{10,... | collective-permute-start | bytes 24584 | tf_op jit(solution)/shard_map/ppermute | solution.py:45
  58.9 3.7 %collective-permute-start.18 = (f32[16,128]{1,0:T(8,128)S(1)}, f32[16,128]{1,0:T(8,128)S(1)}, u32[]{:S(2)}, u32[]{:S(2)}) collective-permute-start(f32[16,128]{1,0:T(8,128)S(1)} %slice.147), channel_id=1, source_target_pairs={{0,1},{1,0},{2,3},{3,2},{4,5},{5,4},{6,7},{7,6},{8,9},{9,8},{10,11... | collective-permute-start | bytes 24584 | tf_op jit(solution)/shard_map/ppermute | solution.py:45
  62.9 4.1 %collective-permute-start.23 = (f32[80,128]{1,0:T(8,128)S(1)}, f32[80,128]{1,0:T(8,128)S(1)}, u32[]{:S(2)}, u32[]{:S(2)}) collective-permute-start(f32[80,128]{1,0:T(8,128)S(1)} %dots.1), channel_id=1, source_target_pairs={{0,192},{4,196},{8,200},{12,204},{16,208},{20,212},{24,216},{28,22... | collective-permute-start | bytes 122888 | tf_op jit(solution)/shard_map/ppermute | solution.py:37
  63.3 3.8 %collective-permute-start.22 = (f32[80,128]{1,0:T(8,128)S(1)}, f32[80,128]{1,0:T(8,128)S(1)}, u32[]{:S(2)}, u32[]{:S(2)}) collective-permute-start(f32[80,128]{1,0:T(8,128)S(1)} %dots.1), channel_id=1, source_target_pairs={{0,64},{4,68},{8,72},{12,76},{16,80},{20,84},{24,88},{28,92},{32,9... | collective-permute-start | bytes 122888 | tf_op jit(solution)/shard_map/ppermute | solution.py:37
  63.3 5.4 %collective-permute-start.21 = (f32[80,128]{1,0:T(8,128)S(1)}, f32[80,128]{1,0:T(8,128)S(1)}, u32[]{:S(2)}, u32[]{:S(2)}) collective-permute-start(f32[80,128]{1,0:T(8,128)S(1)} %dots.1), channel_id=1, source_target_pairs={{0,128},{4,132},{8,136},{12,140},{16,144},{20,148},{24,152},{28,15... | collective-permute-start | bytes 122888 | tf_op jit(solution)/shard_map/ppermute | solution.py:37
  68.7 3.6 %collective-permute-start.26 = (f32[80,128]{1,0:T(8,128)S(1)}, f32[80,128]{1,0:T(8,128)S(1)}, u32[]{:S(2)}, u32[]{:S(2)}) collective-permute-start(f32[80,128]{1,0:T(8,128)S(1)} %add_add_fusion.1), channel_id=1, source_target_pairs={{0,8},{4,12},{8,0},{12,4},{16,24},{20,28},{24,16},{28,20},{32,40},... | collective-permute-start | bytes 122888 | tf_op jit(solution)/shard_map/ppermute | solution.py:41
  70.0 4.2 %collective-permute-start.25 = (f32[80,128]{1,0:T(8,128)S(1)}, f32[80,128]{1,0:T(8,128)S(1)}, u32[]{:S(2)}, u32[]{:S(2)}) collective-permute-start(f32[80,128]{1,0:T(8,128)S(1)} %add_add_fusion.1), channel_id=1, source_target_pairs={{0,16},{4,20},{8,24},{12,28},{16,0},{20,4},{24,8},{28,12},{32,48},... | collective-permute-start | bytes 122888 | tf_op jit(solution)/shard_map/ppermute | solution.py:41
  70.7 4.9 %collective-permute-start.24 = (f32[80,128]{1,0:T(8,128)S(1)}, f32[80,128]{1,0:T(8,128)S(1)}, u32[]{:S(2)}, u32[]{:S(2)}) collective-permute-start(f32[80,128]{1,0:T(8,128)S(1)} %add_add_fusion.1), channel_id=1, source_target_pairs={{0,24},{4,28},{8,16},{12,20},{16,8},{20,12},{24,0},{28,4},{32,56},... | collective-permute-start | bytes 122888 | tf_op jit(solution)/shard_map/ppermute | solution.py:41
  75.6 5.0 %collective-permute-start.27 = (f32[80,128]{1,0:T(8,128)S(1)}, f32[80,128]{1,0:T(8,128)S(1)}, u32[]{:S(2)}, u32[]{:S(2)}) collective-permute-start(f32[80,128]{1,0:T(8,128)S(1)} %add_add_fusion), channel_id=1, source_target_pairs={{0,48},{4,52},{8,56},{12,60},{16,32},{20,36},{24,40},{28,44},{32,1... | collective-permute-start | bytes 122888 | tf_op jit(solution)/shard_map/ppermute | solution.py:41
  80.7 10.7 %collective-permute-start.28 = (f32[80,128]{1,0:T(8,128)S(1)}, f32[80,128]{1,0:T(8,128)S(1)}, u32[]{:S(2)}, u32[]{:S(2)}) collective-permute-start(f32[80,128]{1,0:T(8,128)S(1)} %add.99.refs_0_), channel_id=1, source_target_pairs={{0,4},{4,0},{8,12},{12,8},{16,20},{20,16},{24,28},{28,24},{32,36},... | collective-permute-start | bytes 122888 | tf_op jit(solution)/shard_map/ppermute | solution.py:29

commit v4 on v3

--- a/solution.py
+++ b/solution.py
@@ -204,7 +204,7 @@
     right, left = along_x(half[:mid], 1), along_x(half[mid:], -1)
     b = f_b[:HALF] + far_b
     far_b = swap_z(b[HALF // 2 :], 1)
-    right, left, rest = lax.optimization_barrier((right, left, rest))
+    right, rest = lax.optimization_barrier((right, rest))
     half = f_a[NZ:HALF] + rest
     right = along_x(jnp.concatenate([half[2 * NZ : 2 * NZ + mid] + right, half[2 * NZ + mid :]]), 1)
     left = along_x(jnp.concatenate([half[:mid], half[mid:NZ] + left]), -1)
@@ -282,7 +282,7 @@
             jax.ShapeDtypeStruct((NTASK, n_t), jnp.float32),
         ),
         name="scores",
-    )(*map(in_vmem, parts), tasks.reshape(1, all_v))
+    )(*map(in_vmem, (*parts, tasks.reshape(1, all_v))))
     return cos_t.T, scores_t.T
 
 

time: 92.9 us -> 92.2 us (level)
    ppermute x12, starting transfers between devices: 20.9 us -> 18.4 us  [swap_z(): return lax.ppermute(a, 'coord', coord_pairs(lambda x, z, c: (x, z ^ d, c)))]
    ppermute x4, waiting for transfers between devices: 7.82 us -> 9.79 us  [along_x(): lax.ppermute(a, 'coord', coord_pairs(lambda x, z, c: ((x + d) % NX, z, c)))]
    ppermute x4, starting transfers between devices: 3.16 us -> 5.06 us  [along_x(): lax.ppermute(a, 'coord', coord_pairs(lambda x, z, c: ((x + d) % NX, z, c)))]
    ppermute x12, waiting for transfers between devices: 9.7 us -> 8.29 us  [swap_z(): return lax.ppermute(a, 'coord', coord_pairs(lambda x, z, c: (x, z ^ d, c)))]
    ppermute x4, waiting for transfers between devices: 3.91 us -> 2.7 us  [to_core(): return lax.ppermute(a, 'coord', coord_pairs(lambda x, z, c: (x, z, 1 - c)))]
  transfers between devices with their start and end apart: 29 -> 29, of which waited for: 17 -> 16; matrix products, arithmetic and copies ran while one was open for 1% -> 1% of each run, Pallas kernels for 0% -> 0%
where the time goes in v4:
time: 92.2 us; the launch traced here: 92.1 us
  starting transfers between devices  48.3 us (52%)
  waiting for transfers between devices  25.3 us (27%)
  Pallas kernels  16.8 us (18%)
    ppermute x12, starting transfers between devices, swap_z(): return lax.ppermute(a, 'coord', coord_pairs(lambda x, z, c: (x, z ^ d, c)))  18.4 us
    pallas_call x1, Pallas kernels, local_features(): pl.pallas_call(functools.partial(feature_kernel, (layers, n_t, n_v, cols,...  15.7 us
    ppermute x4, starting transfers between devices, to_core(): return lax.ppermute(a, 'coord', coord_pairs(lambda x, z, c: (x, z, 1 - c)))  14.5 us
    ppermute x4, waiting for transfers between devices, along_x(): lax.ppermute(a, 'coord', coord_pairs(lambda x, z, c: ((x + d) % NX, z, c)))  9.79 us
    ppermute x12, waiting for transfers between devices, swap_z(): return lax.ppermute(a, 'coord', coord_pairs(lambda x, z, c: (x, z ^ d, c)))  8.29 us
    ppermute x6, starting transfers between devices, swap_x(): return lax.ppermute(a, 'coord', coord_pairs(lambda x, z, c: (x ^ d, z, c)))  6.87 us
    ppermute x4, starting transfers between devices, along_x(): lax.ppermute(a, 'coord', coord_pairs(lambda x, z, c: ((x + d) % NX, z, c)))  5.06 us
    ppermute x3, starting transfers between devices, swap_y(): return lax.ppermute(a, 'dp', [(y, y ^ d) for y in range(NY)])  3.5 us
  transfers between devices with their start and end apart: 29, of which 16 were waited for; matrix products, arithmetic and copies ran while one was open for 1% of the time, Pallas kernels for 0%

profile of v4, /device:TPU:1, one launch (start us, length us, event | category | flops | bytes accessed | tf_op | source)
XLA Modules:
  0.0 92.1 jit_solution(12692805877988883937)
XLA Ops:
  0.6 15.7 %features.1 = (f32[64,112,128]{2,1,0:T(8,128)S(1)}, f32[64,32,128]{2,1,0:T(8,128)S(1)}) custom-call(s32[2,80]{1,0:T(2,128)} %bins_hbm.1, bf16[2,128,256,128]{3,2,1,0:T(8,128)(2,1)} %h_t.1, bf16[2,128,80,256]{3,2,1,0:T(8,128)(2,1)} %bitcast.34, bf16[2,16,256,128]{3,2,1,0:T(8,128)(2,1)} %h_v.1, bf16[2,16,80,256]{3,2,1,0:T(8,128)(2,1)} %bitcast.35, ...), custom_call_target="tpu_custom_call" | custom-call | tf_op jit(solution)/shard_map/features/pallas_call | solution.py:157
  16.4 3.3 %collective-permute-start = (f32[8,112,128]{2,1,0:T(8,128)S(1)}, f32[8,112,128]{2,1,0:T(8,128)S(1)}, u32[]{:S(2)}, u32[]{:S(2)}) collective-permute-start(f32[8,112,128]{2,1,0:T(8,128)S(1)} %slice.96), channel_id=1, source_target_pairs={{0,4},{4,0},{8,12},{12,8},{16,20},{20,16},{24,28},{28,24},{32,36},... | collective-permute-start | bytes 1376264 | tf_op jit(solution)/shard_map/ppermute | solution.py:29
  19.7 0.1 slice.97
  19.8 1.3 %collective-permute-done = f32[8,112,128]{2,1,0:T(8,128)S(1)} collective-permute-done((f32[8,112,128]{2,1,0:T(8,128)S(1)}, f32[8,112,128]{2,1,0:T(8,128)S(1)}, u32[]{:S(2)}, u32[]{:S(2)}) %collective-permute-start) | collective-permute-done | bytes 458784 | tf_op jit(solution)/shard_map/ppermute | solution.py:29
  21.1 0.4 collective-permute-start.2
  21.5 0.1 collective-permute-start.10
  21.8 0.1 collective-permute-start.1
  21.8 2.7 %collective-permute-start.4 = (f32[4,112,128]{2,1,0:T(8,128)S(1)}, f32[4,112,128]{2,1,0:T(8,128)S(1)}, u32[]{:S(2)}, u32[]{:S(2)}) collective-permute-start(f32[4,112,128]{2,1,0:T(8,128)S(1)} %get-tuple-element.25), channel_id=1, source_target_pairs={{0,192},{4,196},{8,200},{12,204},{16,208},{20,212},{24,216},{28,22... | collective-permute-start | bytes 688136 | tf_op jit(solution)/shard_map/ppermute | solution.py:33
  24.5 0.5 collective-permute-done.10
  25.0 0.1 slice_add_fusion.1
  25.1 0.1 collective-permute-start.11
  25.2 4.6 %collective-permute-done.1 = f32[4,112,128]{2,1,0:T(8,128)S(1)} collective-permute-done((f32[4,112,128]{2,1,0:T(8,128)S(1)}, f32[4,112,128]{2,1,0:T(8,128)S(1)}, u32[]{:S(2)}, u32[]{:S(2)}) %collective-permute-start.1) | collective-permute-done | bytes 229408 | tf_op jit(solution)/shard_map/ppermute | solution.py:33
  29.9 0.0 collective-permute-done.2
  29.9 0.2 slice_add_fusion
  30.0 0.0 collective-permute-done.4
  30.1 0.1 slice_add_fusion.7
  30.2 2.2 %collective-permute-start.5 = (f32[8,112,128]{2,1,0:T(8,128)S(1)}, f32[8,112,128]{2,1,0:T(8,128)S(1)}, u32[]{:S(2)}, u32[]{:S(2)}) collective-permute-start(f32[8,112,128]{2,1,0:T(8,128)S(1)} %pad_maximum_fusion.1), channel_id=1, source_target_pairs={{0,192},{4,196},{8,200},{12,204},{16,208},{20,212},{24,216},{28,22... | collective-permute-start | bytes 1376264 | tf_op jit(solution)/shard_map/ppermute | solution.py:33
  32.4 0.1 collective-permute-start.3
  32.5 0.2 collective-permute-done.11
  32.8 4.8 %collective-permute-start.12 = (f32[4,32,128]{2,1,0:T(8,128)S(1)}, f32[4,32,128]{2,1,0:T(8,128)S(1)}, u32[]{:S(2)}, u32[]{:S(2)}) collective-permute-start(f32[4,32,128]{2,1,0:T(8,128)S(1)} %get-tuple-element.26), channel_id=1, source_target_pairs={{0,40},{4,44},{8,32},{12,36},{16,56},{20,60},{24,48},{28,52},{32,8... | collective-permute-start | bytes 196616 | tf_op jit(solution)/shard_map/ppermute | solution.py:41
  37.6 0.3 collective-permute-start.14
  37.9 0.9 %collective-permute-start.13 = (f32[4,32,128]{2,1,0:T(8,128)S(1)}, f32[4,32,128]{2,1,0:T(8,128)S(1)}, u32[]{:S(2)}, u32[]{:S(2)}) collective-permute-start(f32[4,32,128]{2,1,0:T(8,128)S(1)} %get-tuple-element.28), channel_id=1, source_target_pairs={{0,16},{4,20},{8,24},{12,28},{16,0},{20,4},{24,8},{28,12},{32,48},... | collective-permute-start | bytes 196616 | tf_op jit(solution)/shard_map/ppermute | solution.py:41
  38.8 2.3 %collective-permute-done.5 = f32[8,112,128]{2,1,0:T(8,128)S(1)} collective-permute-done((f32[8,112,128]{2,1,0:T(8,128)S(1)}, f32[8,112,128]{2,1,0:T(8,128)S(1)}, u32[]{:S(2)}, u32[]{:S(2)}) %collective-permute-start.5) | collective-permute-done | bytes 458784 | tf_op jit(solution)/shard_map/ppermute | solution.py:33
  41.1 2.9 %collective-permute-done.3 = f32[8,112,128]{2,1,0:T(8,128)S(1)} collective-permute-done((f32[8,112,128]{2,1,0:T(8,128)S(1)}, f32[8,112,128]{2,1,0:T(8,128)S(1)}, u32[]{:S(2)}, u32[]{:S(2)}) %collective-permute-start.3) | collective-permute-done | bytes 458784 | tf_op jit(solution)/shard_map/ppermute | solution.py:33
  44.0 0.1 fusion
  44.1 0.0 copy-start
  44.1 0.1 collective-permute-start.6
  44.2 0.0 collective-permute-done.12
  44.2 0.0 collective-permute-done.14
  44.2 0.0 collective-permute-done.13
  44.3 2.2 %collective-permute-start.15 = (f32[32,128]{1,0:T(8,128)S(1)}, f32[32,128]{1,0:T(8,128)S(1)}, u32[]{:S(2)}, u32[]{:S(2)}) collective-permute-start(f32[32,128]{1,0:T(8,128)S(1)} %get-tuple-element.32), channel_id=1, source_target_pairs={{0,128},{4,132},{8,136},{12,140},{16,144},{20,148},{24,152},{28,15... | collective-permute-start | bytes 49160 | tf_op jit(solution)/shard_map/ppermute | solution.py:37
  46.4 0.8 collective-permute-start.17
  47.2 0.0 collective-permute-start.16
  47.2 1.8 %collective-permute-done.6 = f32[4,112,128]{2,1,0:T(8,128)S(1)} collective-permute-done((f32[4,112,128]{2,1,0:T(8,128)S(1)}, f32[4,112,128]{2,1,0:T(8,128)S(1)}, u32[]{:S(2)}, u32[]{:S(2)}) %collective-permute-start.6) | collective-permute-done | bytes 229408 | tf_op jit(solution)/shard_map/ppermute | solution.py:41
  49.1 4.8 %collective-permute-start.7 = (f32[112,128]{1,0:T(8,128)S(1)}, f32[112,128]{1,0:T(8,128)S(1)}, u32[]{:S(2)}, u32[]{:S(2)}) collective-permute-start(f32[112,128]{1,0:T(8,128)S(1)} %get-tuple-element.29), channel_id=1, source_target_pairs={{0,40},{4,44},{8,32},{12,36},{16,56},{20,60},{24,48},{28,52},{32,8... | collective-permute-start | bytes 172040 | tf_op jit(solution)/shard_map/ppermute | solution.py:41
  53.9 0.3 collective-permute-start.9
  54.2 0.0 collective-permute-done.15
  54.2 0.9 %collective-permute-start.8 = (f32[112,128]{1,0:T(8,128)S(1)}, f32[112,128]{1,0:T(8,128)S(1)}, u32[]{:S(2)}, u32[]{:S(2)}) collective-permute-start(f32[112,128]{1,0:T(8,128)S(1)} %get-tuple-element.31), channel_id=1, source_target_pairs={{0,16},{4,20},{8,24},{12,28},{16,0},{20,4},{24,8},{28,12},{32,48},... | collective-permute-start | bytes 172040 | tf_op jit(solution)/shard_map/ppermute | solution.py:41
  55.1 0.0 collective-permute-done.17
  55.1 0.0 collective-permute-done.16
  55.1 2.8 %collective-permute-start.20 = (f32[16,128]{1,0:T(8,128)S(1)}, f32[16,128]{1,0:T(8,128)S(1)}, u32[]{:S(2)}, u32[]{:S(2)}) collective-permute-start(f32[16,128]{1,0:T(8,128)S(1)} %slice.147), channel_id=1, source_target_pairs={{0,3},{1,2},{2,1},{3,0},{4,7},{5,6},{6,5},{7,4},{8,11},{9,10},{10,... | collective-permute-start | bytes 24584 | tf_op jit(solution)/shard_map/ppermute | solution.py:45
  58.0 0.3 collective-permute-start.19
  58.3 0.0 collective-permute-done.7
  58.3 0.3 collective-permute-start.18
  58.6 0.7 collective-permute-done.9
  59.4 0.0 collective-permute-done.8
  59.4 0.0 collective-permute-done.20.v3
  59.4 2.6 %collective-permute-done.19.v2 = f32[16,128]{1,0:T(8,128)S(1)} collective-permute-done((f32[16,128]{1,0:T(8,128)S(1)}, f32[16,128]{1,0:T(8,128)S(1)}, u32[]{:S(2)}, u32[]{:S(2)}) %collective-permute-start.19) | collective-permute-done | bytes 8224 | tf_op jit(solution)/shard_map/ppermute | solution.py:45
  62.0 0.4 dots.1
  62.3 1.4 %collective-permute-start.23 = (f32[80,128]{1,0:T(8,128)S(1)}, f32[80,128]{1,0:T(8,128)S(1)}, u32[]{:S(2)}, u32[]{:S(2)}) collective-permute-start(f32[80,128]{1,0:T(8,128)S(1)} %dots.1), channel_id=1, source_target_pairs={{0,192},{4,196},{8,200},{12,204},{16,208},{20,212},{24,216},{28,22... | collective-permute-start | bytes 122888 | tf_op jit(solution)/shard_map/ppermute | solution.py:37
  63.8 2.5 %collective-permute-start.21 = (f32[80,128]{1,0:T(8,128)S(1)}, f32[80,128]{1,0:T(8,128)S(1)}, u32[]{:S(2)}, u32[]{:S(2)}) collective-permute-start(f32[80,128]{1,0:T(8,128)S(1)} %dots.1), channel_id=1, source_target_pairs={{0,128},{4,132},{8,136},{12,140},{16,144},{20,148},{24,152},{28,15... | collective-permute-start | bytes 122888 | tf_op jit(solution)/shard_map/ppermute | solution.py:37
  66.2 0.2 collective-permute-done.23
  66.4 0.2 collective-permute-done.22
  66.6 1.5 %collective-permute-done.21 = f32[80,128]{1,0:T(8,128)S(1)} collective-permute-done((f32[80,128]{1,0:T(8,128)S(1)}, f32[80,128]{1,0:T(8,128)S(1)}, u32[]{:S(2)}, u32[]{:S(2)}) %collective-permute-start.21) | collective-permute-done | bytes 40992 | tf_op jit(solution)/shard_map/ppermute | solution.py:37
  68.1 1.2 %collective-permute-start.26 = (f32[80,128]{1,0:T(8,128)S(1)}, f32[80,128]{1,0:T(8,128)S(1)}, u32[]{:S(2)}, u32[]{:S(2)}) collective-permute-start(f32[80,128]{1,0:T(8,128)S(1)} %add_add_fusion.1), channel_id=1, source_target_pairs={{0,8},{4,12},{8,0},{12,4},{16,24},{20,28},{24,16},{28,20},{32,40},... | collective-permute-start | bytes 122888 | tf_op jit(solution)/shard_map/ppermute | solution.py:41
  69.4 0.7 collective-permute-start.25
  70.1 1.7 %collective-permute-start.24 = (f32[80,128]{1,0:T(8,128)S(1)}, f32[80,128]{1,0:T(8,128)S(1)}, u32[]{:S(2)}, u32[]{:S(2)}) collective-permute-start(f32[80,128]{1,0:T(8,128)S(1)} %add_add_fusion.1), channel_id=1, source_target_pairs={{0,24},{4,28},{8,16},{12,20},{16,8},{20,12},{24,0},{28,4},{32,56},... | collective-permute-start | bytes 122888 | tf_op jit(solution)/shard_map/ppermute | solution.py:41
  71.8 1.9 %collective-permute-done.25 = f32[80,128]{1,0:T(8,128)S(1)} collective-permute-done((f32[80,128]{1,0:T(8,128)S(1)}, f32[80,128]{1,0:T(8,128)S(1)}, u32[]{:S(2)}, u32[]{:S(2)}) %collective-permute-start.25) | collective-permute-done | bytes 40992 | tf_op jit(solution)/shard_map/ppermute | solution.py:41
  73.7 1.1 %collective-permute-done.24 = f32[80,128]{1,0:T(8,128)S(1)} collective-permute-done((f32[80,128]{1,0:T(8,128)S(1)}, f32[80,128]{1,0:T(8,128)S(1)}, u32[]{:S(2)}, u32[]{:S(2)}) %collective-permute-start.24) | collective-permute-done | bytes 40992 | tf_op jit(solution)/shard_map/ppermute | solution.py:41
  74.8 2.5 %collective-permute-start.27 = (f32[80,128]{1,0:T(8,128)S(1)}, f32[80,128]{1,0:T(8,128)S(1)}, u32[]{:S(2)}, u32[]{:S(2)}) collective-permute-start(f32[80,128]{1,0:T(8,128)S(1)} %add_add_fusion), channel_id=1, source_target_pairs={{0,48},{4,52},{8,56},{12,60},{16,32},{20,36},{24,40},{28,44},{32,1... | collective-permute-start | bytes 122888 | tf_op jit(solution)/shard_map/ppermute | solution.py:41
  77.3 2.6 %collective-permute-done.27 = f32[80,128]{1,0:T(8,128)S(1)} collective-permute-done((f32[80,128]{1,0:T(8,128)S(1)}, f32[80,128]{1,0:T(8,128)S(1)}, u32[]{:S(2)}, u32[]{:S(2)}) %collective-permute-start.27) | collective-permute-done | bytes 40992 | tf_op jit(solution)/shard_map/ppermute | solution.py:41
  79.9 10.6 %collective-permute-start.28 = (f32[80,128]{1,0:T(8,128)S(1)}, f32[80,128]{1,0:T(8,128)S(1)}, u32[]{:S(2)}, u32[]{:S(2)}) collective-permute-start(f32[80,128]{1,0:T(8,128)S(1)} %add.99.refs_0_), channel_id=1, source_target_pairs={{0,4},{4,0},{8,12},{12,8},{16,20},{20,16},{24,28},{28,24},{32,36},... | collective-permute-start | bytes 122888 | tf_op jit(solution)/shard_map/ppermute | solution.py:29
  90.6 0.9 collective-permute-done.28.refs_1_
  91.4 0.7 scores.1
  (24 shorter events, 0.4 us)
Async XLA Ops:
  16.4 4.8 %collective-permute-start = (f32[8,112,128]{2,1,0:T(8,128)S(1)}, f32[8,112,128]{2,1,0:T(8,128)S(1)}, u32[]{:S(2)}, u32[]{:S(2)}) collective-permute-start(f32[8,112,128]{2,1,0:T(8,128)S(1)} %slice.96), channel_id=1, source_target_pairs={{0,4},{4,0},{8,12},{12,8},{16,20},{20,16},{24,28},{28,24},{32,36},... | collective-permute-start | bytes 1376264 | tf_op jit(solution)/shard_map/ppermute | solution.py:29
  21.1 8.7 %collective-permute-start.2 = (f32[24,112,128]{2,1,0:T(8,128)S(1)}, f32[24,112,128]{2,1,0:T(8,128)S(1)}, u32[]{:S(2)}, u32[]{:S(2)}) collective-permute-start(f32[24,112,128]{2,1,0:T(8,128)S(1)} %slice.97), channel_id=1, source_target_pairs={{0,4},{4,0},{8,12},{12,8},{16,20},{20,16},{24,28},{28,24},{32,36},... | collective-permute-start | bytes 4128776 | tf_op jit(solution)/shard_map/ppermute | solution.py:29
  21.5 3.5 %collective-permute-start.10 = (f32[32,32,128]{2,1,0:T(8,128)S(1)}, f32[32,32,128]{2,1,0:T(8,128)S(1)}, u32[]{:S(2)}, u32[]{:S(2)}) collective-permute-start(f32[32,32,128]{2,1,0:T(8,128)S(1)} %slice.98), channel_id=1, source_target_pairs={{0,4},{4,0},{8,12},{12,8},{16,20},{20,16},{24,28},{28,24},{32,36},... | collective-permute-start | bytes 1572872 | tf_op jit(solution)/shard_map/ppermute | solution.py:29
  21.8 8.1 %collective-permute-start.1 = (f32[4,112,128]{2,1,0:T(8,128)S(1)}, f32[4,112,128]{2,1,0:T(8,128)S(1)}, u32[]{:S(2)}, u32[]{:S(2)}) collective-permute-start(f32[4,112,128]{2,1,0:T(8,128)S(1)} %get-tuple-element.24), channel_id=1, source_target_pairs={{0,64},{4,68},{8,72},{12,76},{16,80},{20,84},{24,88},{28,92},{32,9... | collective-permute-start | bytes 688136 | tf_op jit(solution)/shard_map/ppermute | solution.py:33
  21.8 8.2 %collective-permute-start.4 = (f32[4,112,128]{2,1,0:T(8,128)S(1)}, f32[4,112,128]{2,1,0:T(8,128)S(1)}, u32[]{:S(2)}, u32[]{:S(2)}) collective-permute-start(f32[4,112,128]{2,1,0:T(8,128)S(1)} %get-tuple-element.25), channel_id=1, source_target_pairs={{0,192},{4,196},{8,200},{12,204},{16,208},{20,212},{24,216},{28,22... | collective-permute-start | bytes 688136 | tf_op jit(solution)/shard_map/ppermute | solution.py:33
  25.1 7.6 %collective-permute-start.11 = (f32[16,32,128]{2,1,0:T(8,128)S(1)}, f32[16,32,128]{2,1,0:T(8,128)S(1)}, u32[]{:S(2)}, u32[]{:S(2)}) collective-permute-start(f32[16,32,128]{2,1,0:T(8,128)S(1)} %slice.138), channel_id=1, source_target_pairs={{0,8},{4,12},{8,0},{12,4},{16,24},{20,28},{24,16},{28,20},{32,40},... | collective-permute-start | bytes 786440 | tf_op jit(solution)/shard_map/ppermute | solution.py:41
  30.2 10.9 %collective-permute-start.5 = (f32[8,112,128]{2,1,0:T(8,128)S(1)}, f32[8,112,128]{2,1,0:T(8,128)S(1)}, u32[]{:S(2)}, u32[]{:S(2)}) collective-permute-start(f32[8,112,128]{2,1,0:T(8,128)S(1)} %pad_maximum_fusion.1), channel_id=1, source_target_pairs={{0,192},{4,196},{8,200},{12,204},{16,208},{20,212},{24,216},{28,22... | collective-permute-start | bytes 1376264 | tf_op jit(solution)/shard_map/ppermute | solution.py:33
  32.4 11.5 %collective-permute-start.3 = (f32[8,112,128]{2,1,0:T(8,128)S(1)}, f32[8,112,128]{2,1,0:T(8,128)S(1)}, u32[]{:S(2)}, u32[]{:S(2)}) collective-permute-start(f32[8,112,128]{2,1,0:T(8,128)S(1)} %pad_maximum_fusion), channel_id=1, source_target_pairs={{0,64},{4,68},{8,72},{12,76},{16,80},{20,84},{24,88},{28,92},{32,9... | collective-permute-start | bytes 1376264 | tf_op jit(solution)/shard_map/ppermute | solution.py:33
  32.8 11.4 %collective-permute-start.12 = (f32[4,32,128]{2,1,0:T(8,128)S(1)}, f32[4,32,128]{2,1,0:T(8,128)S(1)}, u32[]{:S(2)}, u32[]{:S(2)}) collective-permute-start(f32[4,32,128]{2,1,0:T(8,128)S(1)} %get-tuple-element.26), channel_id=1, source_target_pairs={{0,40},{4,44},{8,32},{12,36},{16,56},{20,60},{24,48},{28,52},{32,8... | collective-permute-start | bytes 196616 | tf_op jit(solution)/shard_map/ppermute | solution.py:41
  37.6 6.6 %collective-permute-start.14 = (f32[4,32,128]{2,1,0:T(8,128)S(1)}, f32[4,32,128]{2,1,0:T(8,128)S(1)}, u32[]{:S(2)}, u32[]{:S(2)}) collective-permute-start(f32[4,32,128]{2,1,0:T(8,128)S(1)} %get-tuple-element.27), channel_id=1, source_target_pairs={{0,48},{4,52},{8,56},{12,60},{16,32},{20,36},{24,40},{28,44},{32,1... | collective-permute-start | bytes 196616 | tf_op jit(solution)/shard_map/ppermute | solution.py:41
  37.9 6.4 %collective-permute-start.13 = (f32[4,32,128]{2,1,0:T(8,128)S(1)}, f32[4,32,128]{2,1,0:T(8,128)S(1)}, u32[]{:S(2)}, u32[]{:S(2)}) collective-permute-start(f32[4,32,128]{2,1,0:T(8,128)S(1)} %get-tuple-element.28), channel_id=1, source_target_pairs={{0,16},{4,20},{8,24},{12,28},{16,0},{20,4},{24,8},{28,12},{32,48},... | collective-permute-start | bytes 196616 | tf_op jit(solution)/shard_map/ppermute | solution.py:41
  44.1 47.4 %copy-start = (s32[64,1]{0,1:T(1,128)S(1)}, s32[64,1]{0,1:T(1,128)}, u32[]{:S(2)}) copy-start(s32[64,1]{0,1:T(1,128)} %param.13) | copy-start | bytes 772
  44.1 5.0 %collective-permute-start.6 = (f32[4,112,128]{2,1,0:T(8,128)S(1)}, f32[4,112,128]{2,1,0:T(8,128)S(1)}, u32[]{:S(2)}, u32[]{:S(2)}) collective-permute-start(f32[4,112,128]{2,1,0:T(8,128)S(1)} %slice.132), channel_id=1, source_target_pairs={{0,8},{4,12},{8,0},{12,4},{16,24},{20,28},{24,16},{28,20},{32,40},... | collective-permute-start | bytes 688136 | tf_op jit(solution)/shard_map/ppermute | solution.py:41
  44.3 9.9 %collective-permute-start.15 = (f32[32,128]{1,0:T(8,128)S(1)}, f32[32,128]{1,0:T(8,128)S(1)}, u32[]{:S(2)}, u32[]{:S(2)}) collective-permute-start(f32[32,128]{1,0:T(8,128)S(1)} %get-tuple-element.32), channel_id=1, source_target_pairs={{0,128},{4,132},{8,136},{12,140},{16,144},{20,148},{24,152},{28,15... | collective-permute-start | bytes 49160 | tf_op jit(solution)/shard_map/ppermute | solution.py:37
  46.4 8.7 %collective-permute-start.17 = (f32[32,128]{1,0:T(8,128)S(1)}, f32[32,128]{1,0:T(8,128)S(1)}, u32[]{:S(2)}, u32[]{:S(2)}) collective-permute-start(f32[32,128]{1,0:T(8,128)S(1)} %get-tuple-element.33), channel_id=1, source_target_pairs={{0,192},{4,196},{8,200},{12,204},{16,208},{20,212},{24,216},{28,22... | collective-permute-start | bytes 49160 | tf_op jit(solution)/shard_map/ppermute | solution.py:37
  47.2 7.9 %collective-permute-start.16 = (f32[32,128]{1,0:T(8,128)S(1)}, f32[32,128]{1,0:T(8,128)S(1)}, u32[]{:S(2)}, u32[]{:S(2)}) collective-permute-start(f32[32,128]{1,0:T(8,128)S(1)} %get-tuple-element.34), channel_id=1, source_target_pairs={{0,64},{4,68},{8,72},{12,76},{16,80},{20,84},{24,88},{28,92},{32,9... | collective-permute-start | bytes 49160 | tf_op jit(solution)/shard_map/ppermute | solution.py:37
  49.1 9.2 %collective-permute-start.7 = (f32[112,128]{1,0:T(8,128)S(1)}, f32[112,128]{1,0:T(8,128)S(1)}, u32[]{:S(2)}, u32[]{:S(2)}) collective-permute-start(f32[112,128]{1,0:T(8,128)S(1)} %get-tuple-element.29), channel_id=1, source_target_pairs={{0,40},{4,44},{8,32},{12,36},{16,56},{20,60},{24,48},{28,52},{32,8... | collective-permute-start | bytes 172040 | tf_op jit(solution)/shard_map/ppermute | solution.py:41
  53.9 5.4 %collective-permute-start.9 = (f32[112,128]{1,0:T(8,128)S(1)}, f32[112,128]{1,0:T(8,128)S(1)}, u32[]{:S(2)}, u32[]{:S(2)}) collective-permute-start(f32[112,128]{1,0:T(8,128)S(1)} %get-tuple-element.30), channel_id=1, source_target_pairs={{0,48},{4,52},{8,56},{12,60},{16,32},{20,36},{24,40},{28,44},{32,1... | collective-permute-start | bytes 172040 | tf_op jit(solution)/shard_map/ppermute | solution.py:41
  54.2 5.2 %collective-permute-start.8 = (f32[112,128]{1,0:T(8,128)S(1)}, f32[112,128]{1,0:T(8,128)S(1)}, u32[]{:S(2)}, u32[]{:S(2)}) collective-permute-start(f32[112,128]{1,0:T(8,128)S(1)} %get-tuple-element.31), channel_id=1, source_target_pairs={{0,16},{4,20},{8,24},{12,28},{16,0},{20,4},{24,8},{28,12},{32,48},... | collective-permute-start | bytes 172040 | tf_op jit(solution)/shard_map/ppermute | solution.py:41
  55.1 4.2 %collective-permute-start.20 = (f32[16,128]{1,0:T(8,128)S(1)}, f32[16,128]{1,0:T(8,128)S(1)}, u32[]{:S(2)}, u32[]{:S(2)}) collective-permute-start(f32[16,128]{1,0:T(8,128)S(1)} %slice.147), channel_id=1, source_target_pairs={{0,3},{1,2},{2,1},{3,0},{4,7},{5,6},{6,5},{7,4},{8,11},{9,10},{10,... | collective-permute-start | bytes 24584 | tf_op jit(solution)/shard_map/ppermute | solution.py:45
  58.0 4.0 %collective-permute-start.19 = (f32[16,128]{1,0:T(8,128)S(1)}, f32[16,128]{1,0:T(8,128)S(1)}, u32[]{:S(2)}, u32[]{:S(2)}) collective-permute-start(f32[16,128]{1,0:T(8,128)S(1)} %slice.147), channel_id=1, source_target_pairs={{0,2},{1,3},{2,0},{3,1},{4,6},{5,7},{6,4},{7,5},{8,10},{9,11},{10,... | collective-permute-start | bytes 24584 | tf_op jit(solution)/shard_map/ppermute | solution.py:45
  58.3 3.7 %collective-permute-start.18 = (f32[16,128]{1,0:T(8,128)S(1)}, f32[16,128]{1,0:T(8,128)S(1)}, u32[]{:S(2)}, u32[]{:S(2)}) collective-permute-start(f32[16,128]{1,0:T(8,128)S(1)} %slice.147), channel_id=1, source_target_pairs={{0,1},{1,0},{2,3},{3,2},{4,5},{5,4},{6,7},{7,6},{8,9},{9,8},{10,11... | collective-permute-start | bytes 24584 | tf_op jit(solution)/shard_map/ppermute | solution.py:45
  62.3 4.1 %collective-permute-start.23 = (f32[80,128]{1,0:T(8,128)S(1)}, f32[80,128]{1,0:T(8,128)S(1)}, u32[]{:S(2)}, u32[]{:S(2)}) collective-permute-start(f32[80,128]{1,0:T(8,128)S(1)} %dots.1), channel_id=1, source_target_pairs={{0,192},{4,196},{8,200},{12,204},{16,208},{20,212},{24,216},{28,22... | collective-permute-start | bytes 122888 | tf_op jit(solution)/shard_map/ppermute | solution.py:37
  63.8 2.9 %collective-permute-start.22 = (f32[80,128]{1,0:T(8,128)S(1)}, f32[80,128]{1,0:T(8,128)S(1)}, u32[]{:S(2)}, u32[]{:S(2)}) collective-permute-start(f32[80,128]{1,0:T(8,128)S(1)} %dots.1), channel_id=1, source_target_pairs={{0,64},{4,68},{8,72},{12,76},{16,80},{20,84},{24,88},{28,92},{32,9... | collective-permute-start | bytes 122888 | tf_op jit(solution)/shard_map/ppermute | solution.py:37
  63.8 4.4 %collective-permute-start.21 = (f32[80,128]{1,0:T(8,128)S(1)}, f32[80,128]{1,0:T(8,128)S(1)}, u32[]{:S(2)}, u32[]{:S(2)}) collective-permute-start(f32[80,128]{1,0:T(8,128)S(1)} %dots.1), channel_id=1, source_target_pairs={{0,128},{4,132},{8,136},{12,140},{16,144},{20,148},{24,152},{28,15... | collective-permute-start | bytes 122888 | tf_op jit(solution)/shard_map/ppermute | solution.py:37
  68.1 3.6 %collective-permute-start.26 = (f32[80,128]{1,0:T(8,128)S(1)}, f32[80,128]{1,0:T(8,128)S(1)}, u32[]{:S(2)}, u32[]{:S(2)}) collective-permute-start(f32[80,128]{1,0:T(8,128)S(1)} %add_add_fusion.1), channel_id=1, source_target_pairs={{0,8},{4,12},{8,0},{12,4},{16,24},{20,28},{24,16},{28,20},{32,40},... | collective-permute-start | bytes 122888 | tf_op jit(solution)/shard_map/ppermute | solution.py:41
  69.4 4.3 %collective-permute-start.25 = (f32[80,128]{1,0:T(8,128)S(1)}, f32[80,128]{1,0:T(8,128)S(1)}, u32[]{:S(2)}, u32[]{:S(2)}) collective-permute-start(f32[80,128]{1,0:T(8,128)S(1)} %add_add_fusion.1), channel_id=1, source_target_pairs={{0,16},{4,20},{8,24},{12,28},{16,0},{20,4},{24,8},{28,12},{32,48},... | collective-permute-start | bytes 122888 | tf_op jit(solution)/shard_map/ppermute | solution.py:41
  70.1 4.7 %collective-permute-start.24 = (f32[80,128]{1,0:T(8,128)S(1)}, f32[80,128]{1,0:T(8,128)S(1)}, u32[]{:S(2)}, u32[]{:S(2)}) collective-permute-start(f32[80,128]{1,0:T(8,128)S(1)} %add_add_fusion.1), channel_id=1, source_target_pairs={{0,24},{4,28},{8,16},{12,20},{16,8},{20,12},{24,0},{28,4},{32,56},... | collective-permute-start | bytes 122888 | tf_op jit(solution)/shard_map/ppermute | solution.py:41
  74.8 5.2 %collective-permute-start.27 = (f32[80,128]{1,0:T(8,128)S(1)}, f32[80,128]{1,0:T(8,128)S(1)}, u32[]{:S(2)}, u32[]{:S(2)}) collective-permute-start(f32[80,128]{1,0:T(8,128)S(1)} %add_add_fusion), channel_id=1, source_target_pairs={{0,48},{4,52},{8,56},{12,60},{16,32},{20,36},{24,40},{28,44},{32,1... | collective-permute-start | bytes 122888 | tf_op jit(solution)/shard_map/ppermute | solution.py:41
  79.9 11.5 %collective-permute-start.28 = (f32[80,128]{1,0:T(8,128)S(1)}, f32[80,128]{1,0:T(8,128)S(1)}, u32[]{:S(2)}, u32[]{:S(2)}) collective-permute-start(f32[80,128]{1,0:T(8,128)S(1)} %add.99.refs_0_), channel_id=1, source_target_pairs={{0,4},{4,0},{8,12},{12,8},{16,20},{20,16},{24,28},{28,24},{32,36},... | collective-permute-start | bytes 122888 | tf_op jit(solution)/shard_map/ppermute | solution.py:29
